TPU v7x, 128 devices: a whole 4x4x4 slice. The times are simulated.
128 devices in a mesh: face: 4 (over y_hi, core), tile: 32 (over y_lo, x, z).
Axes of the slice: x: 4, y: 4 (y_hi: 2, y_lo: 2; y = y_hi * 2 + y_lo), z: 4, core: 2. Of those that a mesh axis runs over, the one named last changes fastest.
Arguments:
- coarse_features: bfloat16 [3, 128, 1024, 256], P(None, None, ('face', 'tile')), may hold values from -6 to 6
- skip_features: bfloat16 [3, 64, 2048, 512], P(None, None, ('face', 'tile')), may hold values from -6 to 6
- up_weight: bfloat16 [2, 2, 64, 128], replicated, may hold values from -0.5 to 0.5
- up_bias: float32 [64], replicated, may hold values from -3 to 3
- first_weight: bfloat16 [3, 3, 64, 128], replicated, may hold values from -0.1875 to 0.1875
- first_bias: float32 [64], replicated, may hold values from -3 to 3
- second_weight: bfloat16 [3, 3, 64, 64], replicated, may hold values from -0.25 to 0.25
- second_bias: float32 [64], replicated, may hold values from -3 to 3
- head_weight: bfloat16 [8, 64], replicated, may hold values from -0.75 to 0.75
- head_bias: float32 [8], replicated, may hold values from -3 to 3
- land_mask: int32 [2048, 512], P(('face', 'tile')), may hold values from 0 to 1, as said below
- block_target: int32 [8192], P(('face', 'tile')), may hold values from -1 to 5631, as said below
Outputs:
- surface_flux: float32 [3, 8, 2048, 512], P(None, None, ('face', 'tile'))
- ocean_flux: float32 [5632, 3, 8, 128], P(('face', 'tile'))
Inputs may be any that keep to these rules, and one draw needn't show every extreme that they name: `land_mask`: 1 marks sea; every pixel of a block whose block_target is -1 is 0. `block_target`: -1 marks a block without sea; every value 0 to 5631 occurs exactly once; value // 44 is the owner, the device of that index along face+tile; the 64 blocks of one device send at most 1 block to any one owner, and this largest count of 1 is reached; some device has no block at -1.
All inputs are finite; a program needn't handle non-finite values.
Results may differ from a plain program's by a relative error of at most 0.007.
Values may be sent and summed in bfloat16 or wider, within the bound.
No kernel may reach another device: no remote copies, remote signals or barrier semaphores. Data moves between devices by JAX's collectives and lax.ppermute only.
A program may use at most 192 MiB of HBM per device.

v0:
```python
import jax
import jax.numpy as jnp
from jax import lax
from jax.sharding import PartitionSpec as P

BLOCK = 128
WET16 = 11


def broadcast(shard, axis, root):
    mine = lax.axis_index(axis) == root
    return lax.psum(jnp.where(mine, shard, jnp.zeros_like(shard)), axis)


def with_halo(block, sides, width, periodic):
    for axis, dim in sides:
        count = lax.axis_size(axis)
        forward = [(i, i + 1) for i in range(count - 1)]
        if periodic:
            forward.append((count - 1, 0))
        backward = [(target, source) for source, target in forward]
        low = lax.ppermute(
            lax.slice_in_dim(block, block.shape[dim] - width, None, axis=dim), axis, forward
        )
        high = lax.ppermute(lax.slice_in_dim(block, 0, width, axis=dim), axis, backward)
        block = jnp.concatenate([low, block, high], axis=dim)
    return block


def edge_padded(values):
    members, channels, row_count, columns = values.shape
    tile_count = lax.axis_size("tile")
    tile_pos = lax.axis_index("tile")
    last_column = values[:, :, :, columns - 1]
    last_row = values[:, :, row_count - 1, :]
    shared_row = broadcast(last_row, "tile", tile_count - 1)
    row_piece = lax.dynamic_slice_in_dim(shared_row, tile_pos * row_count, row_count, 2)
    stacked = jnp.stack([row_piece, last_column], axis=0)
    beside_all = with_halo(stacked, (("face", 0),), 1, True)
    ghost_column = beside_all[3]
    prior_column = lax.all_gather(beside_all[0], "tile", axis=2, tiled=True)
    ghost_row = jnp.where(tile_pos == tile_count - 1, prior_column, jnp.zeros_like(prior_column))
    zero_column = jnp.zeros((members, channels, row_count, 1), values.dtype)
    widened = jnp.concatenate([zero_column, values, ghost_column[:, :, :, None]], axis=3)
    padded = with_halo(widened, (("tile", 2),), 1, False)
    corner = jnp.zeros((members, channels, 1), values.dtype)
    bottom_extra = jnp.concatenate([corner, ghost_row, corner], axis=2)[:, :, None, :]
    return jnp.concatenate(
        [padded[:, :, : row_count + 1], padded[:, :, row_count + 1 :] + bottom_extra], axis=2
    )


def conv_layer(values, weight, bias):
    row_count = values.shape[2]
    columns = values.shape[3]
    padded = edge_padded(values)
    summed = None
    for row_tap in range(3):
        for col_tap in range(3):
            term = jnp.einsum(
                "oc,bcxy->boxy",
                weight[row_tap, col_tap],
                padded[:, :, row_tap : row_tap + row_count, col_tap : col_tap + columns],
                preferred_element_type=jnp.float32,
            )
            summed = term if summed is None else summed + term
    return jax.nn.silu(summed + bias[None, :, None, None]).astype(jnp.bfloat16)


def shards(
    coarse_features,
    skip_features,
    up_weight,
    up_bias,
    first_weight,
    first_bias,
    second_weight,
    second_bias,
    head_weight,
    head_bias,
    land_mask,
    block_target,
):
    members = coarse_features.shape[0]
    out_channels = up_weight.shape[2]
    flux_count = head_weight.shape[0]
    upsampled = jnp.einsum(
        "aeoc,bcij->boiaje", up_weight, coarse_features, preferred_element_type=jnp.float32
    )
    upsampled = upsampled.reshape(
        members, out_channels, 2 * coarse_features.shape[2], 2 * coarse_features.shape[3]
    )
    upsampled = (upsampled + up_bias[None, :, None, None]).astype(jnp.bfloat16)
    joined = jnp.concatenate([upsampled, skip_features], axis=1)
    first = conv_layer(joined, first_weight, first_bias)
    second = conv_layer(first, second_weight, second_bias)
    surface_flux = (
        jnp.einsum("fc,bcxy->bfxy", head_weight, second, preferred_element_type=jnp.float32)
        + head_bias[None, :, None, None]
    )
    row_count = surface_flux.shape[2]
    columns = surface_flux.shape[3]
    masked = surface_flux * land_mask.astype(jnp.float32)[None, None]
    blocks = (
        masked.reshape(members, flux_count, row_count, columns // BLOCK, BLOCK)
        .transpose(2, 3, 0, 1, 4)
        .reshape(-1, members, flux_count, BLOCK)
    )
    face_count = lax.axis_size("face")
    tile_count = lax.axis_size("tile")
    owner_total = face_count * tile_count
    block_count = block_target.shape[0]
    capacity = block_count * WET16 // 16
    most_sent = (block_count + owner_total - 1) // owner_total
    is_wet = block_target >= 0
    owner_of = jnp.where(is_wet, block_target // capacity, -1)
    positions = jnp.arange(block_count)
    earlier = (
        (owner_of[None, :] == owner_of[:, None])
        & is_wet[None, :]
        & (positions[None, :] < positions[:, None])
    )
    within = jnp.sum(earlier.astype(jnp.int32), axis=1)
    slot_index = jnp.where(is_wet, owner_of * most_sent + within, owner_total * most_sent)
    send_values = (
        jnp.zeros((owner_total * most_sent, members, flux_count, BLOCK), jnp.float32)
        .at[slot_index]
        .set(blocks, mode="drop")
    )
    local_slot = jnp.where(is_wet, block_target - owner_of * capacity, capacity)
    send_slots = (
        jnp.full((owner_total * most_sent,), capacity, jnp.int32)
        .at[slot_index]
        .set(local_slot, mode="drop")
    )
    direct_values = send_values.reshape(owner_total, most_sent, members, flux_count, BLOCK)
    direct_slots = send_slots.reshape(owner_total, most_sent)
    got_values, got_slots = (
        lax.all_to_all(
            direct_values.astype(jnp.bfloat16),
            ("face", "tile"),
            split_axis=0,
            concat_axis=0,
            tiled=True,
        ).astype(direct_values.dtype),
        lax.all_to_all(direct_slots, ("face", "tile"), split_axis=0, concat_axis=0, tiled=True),
    )
    got_values = got_values.reshape(-1, members, flux_count, BLOCK)
    got_slots = got_slots.reshape(-1)
    ocean_flux = (
        jnp.zeros((capacity, members, flux_count, BLOCK), jnp.float32)
        .at[got_slots]
        .set(got_values, mode="drop")
    )
    return (surface_flux, ocean_flux)


def solution(mesh):
    placed = (
        P(None, None, ("face", "tile"), None),
        P(None, None, ("face", "tile"), None),
        P(),
        P(),
        P(),
        P(),
        P(),
        P(),
        P(),
        P(),
        P(("face", "tile"), None),
        P(("face", "tile")),
    )
    return jax.shard_map(
        shards,
        mesh=mesh,
        in_specs=placed,
        out_specs=(P(None, None, ("face", "tile"), None), P(("face", "tile"), None, None, None)),
        check_vma=False,
    )
```

profile of v0, /device:TPU:0, one launch (start us, length us, event | category | flops | bytes accessed | tf_op | source)
XLA Modules:
  0.0 871.8 jit_solution(682543240655852821)
XLA Ops:
  10.9 11.1 %all-to-all-start = ((s32[128,1,1]{2,1,0:T(1,128)}), s32[128,1,1]{2,1,0:T(1,128)S(1)}, u32[]{:S(2)}, u32[]{:S(2)}) async-start(s32[128,1,1]{2,1,0:T(1,128)} %copy.161), calls=%async_computation | async-start | bytes 131072 | tf_op jit(solution)/shard_map/all_to_all | solution.py:146
  29.5 17.6 %copy.149 = f32[3,64,8,2,256,2]{1,5,4,3,2,0:T(2,128)} copy(f32[3,64,8,2,256,2]{4,1,5,3,2,0:T(8,128)} %convolution_bitcast_fusion) | data formatting | bytes 12582912 | tf_op jit(solution)/shard_map/aeoc,bcij->boiaje/transpose | solution.py:87
  47.1 9.7 %copy.150 = f32[3,64,16,512]{3,1,2,0:T(8,128)} copy(f32[3,64,16,512]{1,3,2,0:T(8,128)} %bitcast.217) | data formatting | bytes 12582912 | tf_op jit(solution)/shard_map/reshape | solution.py:90
  68.2 4.4 fusion.74
  72.8 5.2 fusion
  78.0 9.2 %copy.154 = bf16[3,128,16,512]{1,2,3,0:T(8,128)(2,1)} copy(bf16[3,128,16,512]{3,1,2,0:T(8,128)(2,1)} %copy-done.6) | data formatting | bytes 12582912 | tf_op jit(solution)/shard_map/concatenate | solution.py:94
  87.2 88.3 %all-gather = bf16[1,3,128,512]{2,3,1,0:T(8,128)(2,1)} all-gather(bf16[1,3,128,16]{2,3,1,0:T(8,128)(2,1)S(1)} %collective-permute-done.3), channel_id=2, replica_groups=mesh['face'=4,'tile'=32] {'tile'}, dimensions={3}, use_global_device_ids=true | all-gather | bytes 405504 | tf_op jit(solution)/shard_map/all_gather | solution.py:41
  177.5 184.3 %all-reduce.5.cloned.1.call-done = bf16[3,128,512]{2,1,0:T(8,128)(2,1)} async-done(((bf16[3,128,512]{2,1,0:T(8,128)(2,1)}), bf16[3,128,512]{2,1,0:T(8,128)(2,1)}) %all-reduce.5.cloned.1.call-update) | async-done | bytes 393232 | tf_op jit(solution)/shard_map/psum | solution.py:12
  362.8 10.5 %collective-permute-start = (bf16[1,3,128,16]{2,3,1,0:T(8,128)(2,1)S(1)}, bf16[1,3,128,16]{2,3,1,0:T(8,128)(2,1)S(1)}, u32[]{:S(2)}, u32[]{:S(2)}) collective-permute-start(bf16[1,3,128,16]{2,3,1,0:T(8,128)(2,1)S(1)} %bitcast.226), channel_id=1, source_target_pairs={{32,0},{64,32},{96,64},{0,96},{33,1},{65,33},{97,65},{1,97},{34,2}... | collective-permute-start | bytes 36872 | tf_op jit(solution)/shard_map/ppermute | solution.py:25
  383.8 5.5 fusion.19
  389.3 6.9 collective-permute-done.2
  396.6 17.8 %maximum_maximum_fusion = (bf16[3,128,17,514]{3,1,2,0:T(8,128)(2,1)S(1)}, bf16[3,128,17,514]{3,1,2,0:T(8,128)(2,1)S(1)}) fusion(bf16[3,128,16,1]{3,1,2,0:T(8,128)(2,1)} %copy.153, bf16[3,64,16,512]{3,1,2,0:T(8,128)(2,1)S(1)} %copy.151, bf16[3,64,16,512]{3,1,2,0:T(8,128)(2,1)S(1)} %copy-done.4, bf16[3,128,16,1]{3,1,2,0:T(8,128)(2,1)} %copy-done.7, ...), kind=kLoop, calls=%fused_computation.3 | loop fusion | flops 67107840 | bytes 20527104 | tf_op jit(solution)/shard_map/concatenate | solution.py:26
  414.4 5.1 fusion.7
  419.5 4.5 fusion.9
  427.6 4.6 fusion.3
  435.9 19.8 %fusion.21 = bf16[3,64,16,512]{3,1,2,0:T(8,128)(2,1)S(1)} fusion(f32[3,16,512,64]{2,3,1,0:T(8,128)} %fusion.3, f32[3,16,512,64]{2,3,1,0:T(8,128)} %fusion.5, f32[3,16,512,64]{2,3,1,0:T(8,128)} %fusion.19, f32[3,16,512,64]{2,3,1,0:T(8,128)} %fusion.74, f32[3,16,512,64]{2,3,1,0:T(8,128)} %fusion, f32[3,16,512,64]{2,3,1,0:T(8,128)S(1)} %bitcast.219, ...), kind=kOutput, calls=%fused_computation.38 | convolution fusion | flops 424673280 | bytes 59785728 | tf_op jit(solution)/shard_map/oc,bcxy->boxy/dot_general | solution.py:60
  463.0 84.2 %all-gather.1 = bf16[1,3,64,512]{2,3,1,0:T(8,128)(2,1)} all-gather(bf16[1,3,64,16]{2,3,1,0:T(8,128)(2,1)S(1)} %collective-permute-done.7), channel_id=3, replica_groups=mesh['face'=4,'tile'=32] {'tile'}, dimensions={3}, use_global_device_ids=true | all-gather | bytes 202752 | tf_op jit(solution)/shard_map/all_gather | solution.py:41
  549.0 208.5 %all-reduce.7.cloned.1.call-done = bf16[3,64,512]{2,1,0:T(8,128)(2,1)} async-done(((bf16[3,64,512]{2,1,0:T(8,128)(2,1)}), bf16[3,64,512]{2,1,0:T(8,128)(2,1)}) %all-reduce.7.cloned.1.call-update) | async-done | bytes 196624 | tf_op jit(solution)/shard_map/psum | solution.py:12
  765.7 4.7 fusion.30
  773.6 6.2 maximum_maximum_fusion.1
  801.9 18.6 %fusion.46 = f32[3,8,16,512]{3,1,2,0:T(8,128)} fusion(f32[3,16,512,64]{2,3,1,0:T(8,128)} %fusion.24, f32[3,16,512,64]{2,3,1,0:T(8,128)} %fusion.26, f32[3,16,512,64]{2,3,1,0:T(8,128)} %fusion.28, f32[3,16,512,64]{2,3,1,0:T(8,128)} %fusion.30, f32[3,16,512,64]{2,3,1,0:T(8,128)} %fusion.59, f32[3,16,512,64]{2,3,1,0:T(8,128)} %fusion.32, ...), kind=kOutput, calls=%fused_computation.65 | convolution fusion | flops 248709120 | bytes 54283264 | tf_op jit(solution)/shard_map/fc,bcxy->bfxy/dot_general | solution.py:98
  825.7 16.9 %all-to-all-start.1 = ((bf16[128,1,3,8,128]{4,3,2,1,0:T(8,128)(2,1)}), bf16[128,1,3,8,128]{4,3,2,1,0:T(8,128)(2,1)S(1)}, u32[]{:S(2)}, u32[]{:S(2)}) async-start(bf16[128,1,3,8,128]{4,3,2,1,0:T(8,128)(2,1)} %convert_bitcast_fusion), calls=%async_computation.1 | async-start | bytes 1572864 | tf_op jit(solution)/shard_map/all_to_all | solution.py:139
  846.4 12.6 %all-to-all-done.1 = bf16[128,1,3,8,128]{4,3,2,1,0:T(8,128)(2,1)S(1)} async-done(((bf16[128,1,3,8,128]{4,3,2,1,0:T(8,128)(2,1)}), bf16[128,1,3,8,128]{4,3,2,1,0:T(8,128)(2,1)S(1)}, u32[]{:S(2)}, u32[]{:S(2)}) %all-to-all-start.1) | async-done | bytes 786464 | tf_op jit(solution)/shard_map/all_to_all | solution.py:139
  859.1 4.8 scatter_fusion.1
  (124 shorter events, 95.9 us)
Async XLA Ops:
  7.2 18.7 %copy-start = (bf16[2,2,64,128]{3,2,1,0:T(8,128)(2,1)S(1)}, bf16[2,2,64,128]{3,2,1,0:T(8,128)(2,1)}, u32[]{:S(2)}) copy-start(bf16[2,2,64,128]{3,2,1,0:T(8,128)(2,1)} %param.14) | copy-start | bytes 196612
  10.9 814.8 %all-to-all-start = ((s32[128,1,1]{2,1,0:T(1,128)}), s32[128,1,1]{2,1,0:T(1,128)S(1)}, u32[]{:S(2)}, u32[]{:S(2)}) async-start(s32[128,1,1]{2,1,0:T(1,128)} %copy.161), calls=%async_computation | async-start | bytes 131072 | tf_op jit(solution)/shard_map/all_to_all | solution.py:146
  22.1 339.7 %all-reduce.5.cloned.1.call-start = ((), (), s32[]{:S(2)}) async-start(), calls=%async_computation.2 | async-start | bytes 786432 | tf_op jit(solution)/shard_map/psum | solution.py:12
  47.1 9.7 %copy-start.20 = (f32[64]{0:T(128)S(1)}, f32[64]{0:T(128)}, u32[]{:S(2)}) copy-start(f32[64]{0:T(128)} %param.15) | copy-start | bytes 772
  63.5 23.7 %collective-permute-start.3 = (bf16[1,3,128,16]{2,3,1,0:T(8,128)(2,1)S(1)}, bf16[1,3,128,16]{2,3,1,0:T(8,128)(2,1)S(1)}, u32[]{:S(2)}, u32[]{:S(2)}) collective-permute-start(bf16[1,3,128,16]{2,3,1,0:T(8,128)(2,1)S(1)} %bitcast.230), channel_id=1, source_target_pairs={{0,32},{32,64},{64,96},{96,0},{1,33},{33,65},{65,97},{97,1},{2,34}... | collective-permute-start | bytes 36872 | tf_op jit(solution)/shard_map/ppermute | solution.py:22
  65.3 692.2 %all-reduce.7.cloned.1.call-start = ((), (), s32[]{:S(2)}) async-start(), calls=%async_computation.3 | async-start | bytes 393216 | tf_op jit(solution)/shard_map/psum | solution.py:12
  78.0 9.2 %copy-start.15 = (s32[16,512]{1,0:T(8,128)S(1)}, s32[16,512]{1,0:T(8,128)}, u32[]{:S(2)}) copy-start(s32[16,512]{1,0:T(8,128)} %param.22) | copy-start | bytes 98308
  362.8 11.9 %collective-permute-start = (bf16[1,3,128,16]{2,3,1,0:T(8,128)(2,1)S(1)}, bf16[1,3,128,16]{2,3,1,0:T(8,128)(2,1)S(1)}, u32[]{:S(2)}, u32[]{:S(2)}) collective-permute-start(bf16[1,3,128,16]{2,3,1,0:T(8,128)(2,1)S(1)} %bitcast.226), channel_id=1, source_target_pairs={{32,0},{64,32},{96,64},{0,96},{33,1},{65,33},{97,65},{1,97},{34,2}... | collective-permute-start | bytes 36872 | tf_op jit(solution)/shard_map/ppermute | solution.py:25
  376.3 6.9 slice-start.2
  376.7 6.6 slice-start.3
  379.1 17.5 %collective-permute-start.1 = (bf16[3,128,1,514]{3,1,2,0:T(8,128)(2,1)S(1)}, bf16[3,128,1,514]{3,1,2,0:T(8,128)(2,1)}, u32[]{:S(2)}, u32[]{:S(2)}) collective-permute-start(bf16[3,128,1,514]{3,1,2,0:T(8,128)(2,1)S(1)} %get-tuple-element.22), channel_id=1, source_target_pairs={{0,1},{1,2},{2,3},{3,4},{4,5},{5,6},{6,7},{7,8},{8,9},{9,10},{10,1... | collective-permute-start | bytes 1184264 | tf_op jit(solution)/shard_map/ppermute | solution.py:22
  381.8 14.4 %collective-permute-start.2 = (bf16[3,128,1,514]{3,1,2,0:T(8,128)(2,1)S(1)}, bf16[3,128,1,514]{3,1,2,0:T(8,128)(2,1)S(1)}, u32[]{:S(2)}, u32[]{:S(2)}) collective-permute-start(bf16[3,128,1,514]{3,1,2,0:T(8,128)(2,1)S(1)} %get-tuple-element.23), channel_id=1, source_target_pairs={{1,0},{2,1},{3,2},{4,3},{5,4},{6,5},{7,6},{8,7},{9,8},{10,9},{11,1... | collective-permute-start | bytes 1184264 | tf_op jit(solution)/shard_map/ppermute | solution.py:25
  383.8 12.4 %copy-start.11 = (bf16[3,128,512]{2,1,0:T(8,128)(2,1)S(1)}, bf16[3,128,512]{2,1,0:T(8,128)(2,1)}, u32[]{:S(2)}) copy-start(bf16[3,128,512]{2,1,0:T(8,128)(2,1)} %select_bitcast_fusion) | copy-start | bytes 1179652
  383.8 12.7 %copy-start.4 = (bf16[3,64,16,512]{3,1,2,0:T(8,128)(2,1)S(1)}, bf16[3,64,16,512]{3,1,2,0:T(8,128)(2,1)}, u32[]{:S(2)}) copy-start(bf16[3,64,16,512]{3,1,2,0:T(8,128)(2,1)} %copy-done.2) | copy-start | bytes 9437188
  414.4 17.8 %copy-start.5 = (bf16[3,128,17,514]{3,1,2,0:T(8,128)(2,1)}, bf16[3,128,17,514]{3,1,2,0:T(8,128)(2,1)S(1)}, u32[]{:S(2)}) copy-start(bf16[3,128,17,514]{3,1,2,0:T(8,128)(2,1)S(1)} %get-tuple-element.21) | copy-start | bytes 20132356
  427.6 8.2 slice-start
  457.1 5.9 collective-permute-start.7
  758.5 1.4 collective-permute-start.4
  762.5 11.1 %collective-permute-start.5 = (bf16[3,64,1,514]{3,1,2,0:T(8,128)(2,1)S(1)}, bf16[3,64,1,514]{3,1,2,0:T(8,128)(2,1)S(1)}, u32[]{:S(2)}, u32[]{:S(2)}) collective-permute-start(bf16[3,64,1,514]{3,1,2,0:T(8,128)(2,1)S(1)} %get-tuple-element.26), channel_id=1, source_target_pairs={{0,1},{1,2},{2,3},{3,4},{4,5},{5,6},{6,7},{7,8},{8,9},{9,10},{10,1... | collective-permute-start | bytes 592136 | tf_op jit(solution)/shard_map/ppermute | solution.py:22
  764.4 9.0 %collective-permute-start.6 = (bf16[3,64,1,514]{3,1,2,0:T(8,128)(2,1)S(1)}, bf16[3,64,1,514]{3,1,2,0:T(8,128)(2,1)S(1)}, u32[]{:S(2)}, u32[]{:S(2)}) collective-permute-start(bf16[3,64,1,514]{3,1,2,0:T(8,128)(2,1)S(1)} %get-tuple-element.27), channel_id=1, source_target_pairs={{1,0},{2,1},{3,2},{4,3},{5,4},{6,5},{7,6},{8,7},{9,8},{10,9},{11,1... | collective-permute-start | bytes 592136 | tf_op jit(solution)/shard_map/ppermute | solution.py:25
  773.6 6.2 copy-start.13
  820.5 24.5 %copy-start.10 = (f32[3,8,16,512]{3,1,2,0:T(8,128)S(1)}, f32[3,8,16,512]{3,1,2,0:T(8,128)}, u32[]{:S(2)}) copy-start(f32[3,8,16,512]{3,1,2,0:T(8,128)} %fusion.46) | copy-start | bytes 2359300
  822.0 42.7 %copy-start.1 = (bf16[2,2,64,128]{3,2,1,0:T(8,128)(2,1)S(1)}, bf16[2,2,64,128]{3,2,1,0:T(8,128)(2,1)}, u32[]{:S(2)}) copy-start(bf16[2,2,64,128]{3,2,1,0:T(8,128)(2,1)} %param.14) | copy-start | bytes 196612
  825.7 33.3 %all-to-all-start.1 = ((bf16[128,1,3,8,128]{4,3,2,1,0:T(8,128)(2,1)}), bf16[128,1,3,8,128]{4,3,2,1,0:T(8,128)(2,1)S(1)}, u32[]{:S(2)}, u32[]{:S(2)}) async-start(bf16[128,1,3,8,128]{4,3,2,1,0:T(8,128)(2,1)} %convert_bitcast_fusion), calls=%async_computation.1 | async-start | bytes 1572864 | tf_op jit(solution)/shard_map/all_to_all | solution.py:139
  (13 other events, 43.5 us)
Sparse Core Ops, SparseCore 0:
  65.5 296.2 all-reduce.4
  458.8 298.6 all-reduce.6
where the time goes:
time: 881 us; the launch traced here: 872 us
  waiting for transfers between devices  417 us (47%)
  blocking collectives  172 us (20%)
  matrix products  110 us (12%)
  local copies, waits for them, and re-layouts  63.7 us (7%)
  starting transfers between devices  47.6 us (5%)
  other arithmetic  46.3 us (5%)
  between operations  14.7 us (2%)
    psum x2, waiting for transfers between devices, broadcast(): return lax.psum(jnp.where(mine, shard, jnp.zeros_like(shard)), axis)  393 us
    all_gather x2, blocking collectives, edge_padded(): prior_column = lax.all_gather(beside_all[0], 'tile', axis=2, tiled=True)  172 us
    dot_general x17, matrix products, conv_layer(): jnp.einsum('oc,bcxy->boxy', weight[row_tap, col_tap], padded[:, :, row_ta...  87.4 us
    concatenate x2, other arithmetic, with_halo(): block = jnp.concatenate([low, block, high], axis=dim)  24 us
    dot_general x1, matrix products, shards(): jnp.einsum('fc,bcxy->bfxy', head_weight, second, preferred_element_type=j...  18.6 us
  transfers between devices with their start and end apart: 12, of which 7 were waited for; matrix products, arithmetic and copies ran while one was open for 24% of the time, Pallas kernels for 0%

commit v1 on v0

v1 whole, which is shorter than its diff:
```python
import jax
import jax.numpy as jnp
from jax import lax
from jax.experimental import pallas as pl
from jax.experimental.pallas import tpu as pltpu
from jax.sharding import PartitionSpec as P

BF = jnp.bfloat16
F32 = jnp.float32
ROWS = 16
COLS = 512
BLOCK = 128
CAP = 44
VMEM_LIMIT = 56 * 1024 * 1024


def dot(a, b):
    return jnp.dot(a, b, preferred_element_type=F32)


def silu(v):
    half = 0.5 * v
    return half * jnp.tanh(half) + half


def lanes_of(shape):
    return lax.broadcasted_iota(jnp.int32, shape, len(shape) - 1)


def wide(column, tiles):
    return jnp.concatenate([column] * tiles, axis=1)


def taps(row):
    lane = lanes_of(row.shape)
    zero = jnp.zeros_like(row)
    before = jnp.where(lane == 0, zero, pltpu.roll(row, 1, 1))
    after = jnp.where(lane == COLS - 1, zero, pltpu.roll(row, COLS - 1, 1))
    return jnp.concatenate([before, row, after], axis=0)


def spread(coarse):
    lane = lanes_of((128, 128))
    parts = [
        jnp.take_along_axis(coarse[:, 128 * p : 128 * p + 128], lane // 2 + 64 * h, axis=1)
        for p in range(2)
        for h in range(2)
    ]
    even = lane % 2 == 0
    zero = jnp.zeros((128, 128), F32)
    top = jnp.concatenate([jnp.where(even, part, zero) for part in parts], axis=1)
    low = jnp.concatenate([jnp.where(even, zero, part) for part in parts], axis=1)
    return jnp.concatenate([top, low], axis=0).astype(BF)


def up_rows(up_ref):
    return jnp.concatenate(
        [jnp.concatenate([up_ref[a, 0], up_ref[a, 1]], axis=1) for a in range(2)], axis=0
    )


def row_taps(weight_ref, r):
    return jnp.concatenate([weight_ref[r, s] for s in range(3)], axis=1)


def turned_taps(weight_ref, r):
    return jnp.concatenate([weight_ref[s, 2 - r] for s in range(3)], axis=1)


def pack_kernel(coarse_ref, skip_ref, up_ref, down_ref, send_ref, col_ref, row_ref, skip_t, coarse_t):
    last_tile = lax.axis_size("tile") - 1
    tile = lax.axis_index("tile")
    rows = jnp.swapaxes(skip_ref[0], 0, 1)
    coarse_rows = jnp.swapaxes(coarse_ref[0], 0, 1)

    def pair(row):
        return jnp.concatenate([row[:64], row[64:]], axis=1)

    up_ref[0, 0] = rows[0]
    up_ref[0, 1] = rows[1]
    up_ref[0, 2] = pair(coarse_rows[0])
    down_ref[0, 0] = rows[14]
    down_ref[0, 1] = rows[15]
    down_ref[0, 2] = pair(coarse_rows[7])

    lane = lanes_of((128, 128))
    skip_cols = jnp.zeros((128, 128), F32)
    coarse_cols = jnp.zeros((128, 128), F32)
    for x in range(ROWS):
        end = rows[x][:, 384:512].astype(F32)
        both = jnp.concatenate([pltpu.roll(end, x + 1, 1), pltpu.roll(end, x + 2, 1)], axis=0)
        skip_cols = jnp.where(lane == x, both, skip_cols)
    for i in range(ROWS // 2):
        end = coarse_rows[i][:, 128:256].astype(F32)
        coarse_cols = jnp.where(lane == i, pltpu.roll(end, i + 1, 1), coarse_cols)
    piece = jnp.concatenate([skip_cols.T[:16], coarse_cols.T[:16]], axis=0).astype(BF)
    col_ref[...] = piece
    send_ref[31] = piece

    @pl.when(tile == last_tile)
    def _():
        skip_t[...] = jnp.zeros_like(skip_t)
        coarse_t[...] = jnp.zeros_like(coarse_t)
        both = jnp.concatenate([rows[15], rows[14]], axis=0).astype(F32)
        for q in range(4):
            skip_t[8 + 128 * q : 136 + 128 * q, :] = both[:, 128 * q : 128 * q + 128].T
        below = coarse_rows[7].astype(F32)
        for q in range(2):
            coarse_t[8 + 128 * q : 136 + 128 * q, :] = below[:, 128 * q : 128 * q + 128].T
        for j in range(32):
            part = jnp.concatenate(
                [
                    skip_t[16 * j + 6 : 16 * j + 26, :],
                    coarse_t[8 * j + 7 : 8 * j + 19, :],
                ],
                axis=0,
            ).astype(BF)
            if j < 31:
                send_ref[j] = part
            else:
                row_ref[...] = part

    @pl.when(tile != last_tile)
    def _():
        row_ref[...] = jnp.zeros_like(row_ref)


def inner_kernel(coarse_ref, skip_ref, up_w_ref, w_ref, bias_ref, first_ref, part_ref, edge_ref, last_ref):
    last_tile = lax.axis_size("tile") - 1
    bottom = lax.axis_index("tile") == last_tile
    rows = jnp.swapaxes(skip_ref[0], 0, 1)
    coarse_rows = jnp.swapaxes(coarse_ref[0], 0, 1)
    up_w = up_rows(up_w_ref)
    up_bias = wide(bias_ref[0], 4)
    first_bias = wide(bias_ref[1], 4)
    by_row = [row_taps(w_ref, r) for r in range(3)]
    weight = jnp.concatenate(by_row, axis=0)
    turned = jnp.where(bottom, turned_taps(w_ref, 0), by_row[0])
    last_weight = jnp.concatenate([turned, by_row[1], by_row[2]], axis=0)
    lane = lanes_of((128, 128))
    lane64 = lanes_of((64, 128))
    ends = jnp.zeros((128, 128), F32)
    last = jnp.zeros((64, 128), F32)
    before = [None, None]
    for k in range(ROWS // 2):
        fine = dot(up_w, spread(coarse_rows[k].astype(F32)))
        for a in range(2):
            i = 2 * k + a
            upsampled = (fine[64 * a : 64 * a + 64] + up_bias).astype(BF)
            row = jnp.concatenate([upsampled, rows[i]], axis=0)
            end = row[:, 384:512].astype(F32)
            ends = jnp.where(lane == i + 2, pltpu.roll(end, i + 3, 1), ends)
            summed = dot(last_weight if i == ROWS - 1 else weight, taps(row))
            low, mid, high = summed[:64], summed[64:128], summed[128:]
            done = high if before[0] is None else before[0] + high
            before = [mid if before[1] is None else before[1] + mid, low]
            if i == 0:
                part_ref[0, 0] = done
            elif i == 1:
                part_ref[0, 1] = done
            else:
                value = done + first_bias
                first_ref[0, i - 1] = silu(value).astype(BF)
                last = jnp.where(lane64 == i + 1, pltpu.roll(value[:, 384:512], i + 2, 1), last)
    part_ref[0, 2] = before[0]
    part_ref[0, 3] = before[1]
    edge_ref[0] = ends
    last_ref[0] = last


def edge_kernel(
    target_ref, first_ref, part_ref, edge_ref, last_ref, above_ref, below_ref, recv_ref, col1_ref, col2_ref,
    row1_ref, up_w_ref, w1_ref, w2_ref, head_ref, bias_ref, head_bias_ref, mask_ref,
    flux_ref, send_ref, halo_skip, halo_coarse, blocks, piece_ref,
):
    member = pl.program_id(0)
    last_tile = lax.axis_size("tile") - 1
    tile = lax.axis_index("tile")
    bottom = tile == last_tile
    top = tile == 0
    lane = lanes_of((128, 128))
    lane64 = lanes_of((64, 128))
    base = member * 32

    @pl.when(jnp.logical_not(bottom))
    def _():
        halo_skip[0] = below_ref[0, 0].astype(F32)
        halo_skip[1] = below_ref[0, 1].astype(F32)
        both = below_ref[0, 2].astype(F32)
        halo_coarse[...] = jnp.concatenate([both[:, :256], both[:, 256:]], axis=0)
        piece_ref[...] = recv_ref[31, pl.ds(pl.multiple_of(base, 32), 32), :].astype(F32)

    @pl.when(bottom)
    def _():
        pieces = [recv_ref[j, pl.ds(pl.multiple_of(base, 32), 32), :].astype(F32) for j in range(31)]
        pieces.append(col1_ref[pl.ds(pl.multiple_of(base, 32), 32), :].astype(F32))
        for q in range(4):
            stacked = jnp.concatenate([pieces[8 * q + j][:16] for j in range(8)], axis=0).T
            halo_skip[0, :, 128 * q : 128 * q + 128] = stacked[:64]
            halo_skip[1, :, 128 * q : 128 * q + 128] = stacked[64:]
        for q in range(2):
            stacked = jnp.concatenate([pieces[16 * q + j][16:24] for j in range(16)], axis=0).T
            halo_coarse[:, 128 * q : 128 * q + 128] = stacked
        piece_ref[...] = row1_ref[pl.ds(pl.multiple_of(base, 32), 32), :].astype(F32)

    up_bias = bias_ref[0]
    up_bias_wide = wide(up_bias, 4)
    first_bias = bias_ref[1]
    first_bias_wide = wide(first_bias, 4)
    second_bias_wide = wide(bias_ref[2], 4)
    head_bias = wide(head_bias_ref[...], 4)

    up_w = up_rows(up_w_ref)
    both = above_ref[0, 2].astype(F32)
    fine = dot(up_w, spread(jnp.concatenate([both[:, :256], both[:, 256:]], axis=0)))
    above = []
    for a in range(2):
        upsampled = (fine[64 * a : 64 * a + 64] + up_bias_wide).astype(BF)
        row = jnp.concatenate([upsampled, above_ref[0, a]], axis=0)
        above.append(jnp.where(top, jnp.zeros_like(row), row))
    turned_up = jnp.concatenate(
        [jnp.concatenate([up_w_ref[0, 1 - q], up_w_ref[1, 1 - q]], axis=1) for q in range(2)], axis=0
    )
    fine = dot(jnp.where(bottom, turned_up, up_w), spread(halo_coarse[...]))
    below = []
    for a in range(2):
        upsampled = (fine[64 * a : 64 * a + 64] + up_bias_wide).astype(BF)
        below.append(jnp.concatenate([upsampled, halo_skip[a].astype(BF)], axis=0))

    pixel = tile * ROWS - 2 + lane
    piece = jnp.concatenate([piece_ref[...], jnp.zeros((96, 128), F32)], axis=0).T
    doubled = jnp.take_along_axis(piece, jnp.minimum(20 + lane // 2, 127), axis=1)
    even = lane % 2 == 0
    zero = jnp.zeros((128, 128), F32)
    spread_piece = jnp.concatenate(
        [jnp.where(even, doubled, zero), jnp.where(even, zero, doubled)], axis=0
    ).astype(BF)
    ghost_up = jnp.concatenate(
        [jnp.concatenate([up_w_ref[1 - q, 0], up_w_ref[1 - q, 1]], axis=1) for q in range(2)], axis=0
    )
    ghost_fine = dot(ghost_up, spread_piece)
    inside = (lane < 20) & (pixel >= 0) & (pixel < COLS)
    ghost = []
    for q in range(2):
        upsampled = (ghost_fine[64 * q : 64 * q + 64] + up_bias).astype(BF).astype(F32)
        column = jnp.concatenate([upsampled, piece[64 * q : 64 * q + 64]], axis=0)
        ghost.append(jnp.where(inside, column, zero))

    corner = jnp.concatenate(
        [col2_ref[pl.ds(pl.multiple_of(base, 32), 32), :].astype(F32), jnp.zeros((96, 128), F32)], axis=0
    ).T
    corner_bf = corner.astype(BF)

    def corner_column(a, e, q, x):
        upsampled = (dot(up_w_ref[a, e], corner_bf) + up_bias).astype(BF).astype(F32)
        column = jnp.concatenate(
            [pltpu.roll(upsampled, 123, 1), pltpu.roll(corner[64 * q : 64 * q + 64], 18 - x, 1)], axis=0
        )
        return jnp.where((lane == 18) & bottom, column, zero)

    corner0 = corner_column(1, 1, 0, 15)
    corner1 = corner_column(1, 0, 1, 15)
    corner2 = corner_column(0, 1, 0, 14)

    ghost_bf = ghost[0].astype(BF)
    around = jnp.concatenate(
        [pltpu.roll(ghost_bf, 1, 1), ghost_bf, pltpu.roll(ghost_bf, 127, 1)], axis=0
    )
    weight = jnp.concatenate([w1_ref[r, 2] for r in range(3)], axis=1)
    added = dot(weight, around)
    weight = jnp.concatenate([w1_ref[2, 1], w1_ref[2, 0]], axis=1)
    added_bottom = dot(weight, jnp.concatenate([corner0, corner2], axis=0).astype(BF))
    added = jnp.where((lane64 == 18) & bottom, added_bottom, added)

    edge = edge_ref[0]
    for x, row in ((0, above[0]), (1, above[1]), (18, below[0]), (19, below[1])):
        end = pltpu.roll(row[:, 384:512].astype(F32), (x + 1) % 128, 1)
        edge = jnp.where(lane == x, end, edge)
    edge = jnp.where((lane == 18) & bottom, zero, edge)
    columns = [edge.astype(BF), (ghost[0] + corner0).astype(BF), (ghost[1] + corner1).astype(BF)]
    around = jnp.concatenate(
        [part for column in columns for part in (pltpu.roll(column, 1, 1), column, pltpu.roll(column, 127, 1))],
        axis=0,
    )
    weight = jnp.concatenate([w1_ref[2 - s, r] for s in range(3) for r in range(3)], axis=1)
    pixel64 = tile * ROWS - 2 + lane64
    inside64 = (lane64 >= 1) & (lane64 <= 18) & (pixel64 >= 0) & (pixel64 < COLS)
    first_ghost = jnp.where(inside64, silu(dot(weight, around) + first_bias), jnp.zeros((64, 128), F32))
    first_ghost = first_ghost.astype(BF).astype(F32)

    by_row = [row_taps(w1_ref, r) for r in range(3)]
    turned = [jnp.where(bottom, turned_taps(w1_ref, r), by_row[r]) for r in range(3)]
    term = dot(by_row[0], taps(above[0]))
    terms = dot(jnp.concatenate([by_row[1], by_row[0]], axis=0), taps(above[1]))
    row_m1 = part_ref[0, 0] + term + terms[:64]
    row_0 = part_ref[0, 1] + terms[64:]
    term = dot(turned[2], taps(below[1]))
    terms = dot(jnp.concatenate([turned[1], by_row[2]], axis=0), taps(below[0]))
    row_15 = part_ref[0, 2] + terms[64:]
    row_16 = part_ref[0, 3] + term + terms[:64]

    def finished(summed, x):
        end = summed[:, 384:512] + jnp.where(lane64 == 127, pltpu.roll(added, 125 - x, 1), 0.0)
        summed = jnp.concatenate([summed[:, :384], end], axis=1)
        return silu(summed + first_bias_wide).astype(BF)

    row_m1 = finished(row_m1, -1)
    outer = {
        -1: jnp.where(top, jnp.zeros_like(row_m1), row_m1),
        0: finished(row_0, 0),
        15: finished(row_15, 15),
        16: finished(row_16, 16),
    }
    last = silu(last_ref[0] + added).astype(BF).astype(F32)

    weight = jnp.concatenate([row_taps(w2_ref, r) for r in range(3)], axis=0)
    head = head_ref[...]
    before = [None, None]
    lane512 = lanes_of((64, COLS))
    for x in range(-1, ROWS + 1):
        if x in outer:
            row = outer[x]
        else:
            row = first_ref[0, x]
            end = jnp.where(lane64 == 127, pltpu.roll(last, 125 - x, 1).astype(BF), row[:, 384:512])
            row = jnp.concatenate([row[:, :384], end], axis=1)
        moved = pltpu.roll(row, COLS - 1, 1)
        end = jnp.where(lane64 == 127, pltpu.roll(first_ghost, 125 - x, 1).astype(BF), moved[:, 384:512])
        after = jnp.concatenate([moved[:, :384], end], axis=1)
        first_part = jnp.where(lane512 == 0, jnp.zeros_like(row), pltpu.roll(row, 1, 1))
        summed = dot(weight, jnp.concatenate([first_part, row, after], axis=0))
        low, mid, high = summed[:64], summed[64:128], summed[128:]
        done = high if before[0] is None else before[0] + high
        before = [mid if before[1] is None else before[1] + mid, low]
        n = x - 1
        if n >= 0:
            second = silu(done + second_bias_wide).astype(BF)
            flux = dot(head, second) + head_bias
            flux_ref[0, :, n, :] = flux
            masked = flux * mask_ref[n : n + 1, :].astype(F32)
            for q in range(COLS // BLOCK):
                blocks[4 * n + q, pl.ds(pl.multiple_of(member * 8, 8), 8), :] = masked[:, 128 * q : 128 * q + 128]

    @pl.when(member == pl.num_programs(0) - 1)
    def _():
        send_ref[...] = jnp.full(send_ref.shape, -1, BF)

        def place(n, carry):
            target = target_ref[n]

            @pl.when(target >= 0)
            def _():
                owner = lax.div(target, CAP)
                slot = (target - owner * CAP).astype(F32)
                send_ref[owner] = jnp.concatenate(
                    [blocks[n], jnp.full((8, 128), slot, F32)], axis=0
                ).astype(BF)

            return carry

        lax.fori_loop(0, target_ref.shape[0], place, 0)


def unpack_kernel(slot_ref, recv_ref, out_ref):
    def place(n, carry):
        slot = slot_ref[n]

        @pl.when(slot >= 0)
        def _():
            out_ref[slot] = recv_ref[n].astype(F32)[:24]

        return carry

    lax.fori_loop(0, slot_ref.shape[0], place, 0)


def whole(shape):
    return pl.BlockSpec(shape, lambda b: (0,) * len(shape))


def member(shape):
    return pl.BlockSpec((1,) + shape, lambda b: (b,) + (0,) * len(shape))


def shards(
    coarse_features,
    skip_features,
    up_weight,
    up_bias,
    first_weight,
    first_bias,
    second_weight,
    second_bias,
    head_weight,
    head_bias,
    land_mask,
    block_target,
):
    faces = lax.axis_size("face")
    tiles = lax.axis_size("tile")
    devices = faces * tiles
    params = pltpu.CompilerParams(vmem_limit_bytes=VMEM_LIMIT)
    sds = jax.ShapeDtypeStruct

    to_up, to_down, send, col, row = pl.pallas_call(
        pack_kernel,
        grid=(3,),
        in_specs=[member((128, 8, 256)), member((64, 16, 512))],
        out_specs=[
            member((3, 64, 512)),
            member((3, 64, 512)),
            pl.BlockSpec((32, 32, 128), lambda b: (0, b, 0)),
            pl.BlockSpec((32, 128), lambda b: (b, 0)),
            pl.BlockSpec((32, 128), lambda b: (b, 0)),
        ],
        out_shape=[
            sds((3, 3, 64, 512), BF),
            sds((3, 3, 64, 512), BF),
            sds((32, 96, 128), BF),
            sds((96, 128), BF),
            sds((96, 128), BF),
        ],
        scratch_shapes=[pltpu.VMEM((544, 128), F32), pltpu.VMEM((272, 128), F32)],
        compiler_params=params,
        name="pack_edges",
    )(coarse_features, skip_features)

    above = lax.ppermute(to_down, "tile", [(t, t + 1) for t in range(tiles - 1)])
    below = lax.ppermute(to_up, "tile", [(t + 1, t) for t in range(tiles - 1)])
    last = tiles - 1

    def around(step):
        return [(f * tiles + last, ((f + step) % faces) * tiles + last) for f in range(faces)]

    both = ("face", "tile")
    col1 = lax.ppermute(col, both, around(1))
    col2 = lax.ppermute(col, both, around(2))
    row1 = lax.ppermute(row, both, around(faces - 1))
    groups = [
        [f * tiles + t for t in range(last)] + [((f + 1) % faces) * tiles + last] for f in range(faces)
    ]
    recv = lax.all_to_all(send, both, 0, 0, axis_index_groups=groups, tiled=True)

    biases = jnp.broadcast_to(jnp.stack([up_bias, first_bias, second_bias])[:, :, None], (3, 64, 128))
    head_biases = jnp.broadcast_to(head_bias[:, None], (8, 128))

    first, parts, edge, last_col = pl.pallas_call(
        inner_kernel,
        grid=(3,),
        in_specs=[
            member((128, 8, 256)),
            member((64, 16, 512)),
            whole((2, 2, 64, 128)),
            whole((3, 3, 64, 128)),
            whole((3, 64, 128)),
        ],
        out_specs=[member((16, 64, 512)), member((4, 64, 512)), member((128, 128)), member((64, 128))],
        out_shape=[
            sds((3, 16, 64, 512), BF),
            sds((3, 4, 64, 512), F32),
            sds((3, 128, 128), F32),
            sds((3, 64, 128), F32),
        ],
        compiler_params=params,
        cost_estimate=pl.CostEstimate(flops=8 * 10**9, bytes_accessed=9 * 10**6, transcendentals=0),
        name="inner_rows",
    )(coarse_features, skip_features, up_weight, first_weight, biases)

    flux, send = pl.pallas_call(
        edge_kernel,
        grid=(3,),
        in_specs=[
            pl.BlockSpec(memory_space=pltpu.SMEM),
            member((16, 64, 512)),
            member((4, 64, 512)),
            member((128, 128)),
            member((64, 128)),
            member((3, 64, 512)),
            member((3, 64, 512)),
            whole((32, 96, 128)),
            whole((96, 128)),
            whole((96, 128)),
            whole((96, 128)),
            whole((2, 2, 64, 128)),
            whole((3, 3, 64, 128)),
            whole((3, 3, 64, 64)),
            whole((8, 64)),
            whole((3, 64, 128)),
            whole((8, 128)),
            whole((16, 512)),
        ],
        out_specs=[member((8, 16, 512)), whole((128, 32, 128))],
        out_shape=[sds((3, 8, 16, 512), F32), sds((devices, 32, 128), BF)],
        scratch_shapes=[
            pltpu.VMEM((2, 64, 512), F32),
            pltpu.VMEM((128, 256), F32),
            pltpu.VMEM((64, 24, 128), F32),
            pltpu.VMEM((32, 128), F32),
        ],
        compiler_params=params,
        name="edges_and_second",
    )(
        block_target, first, parts, edge, last_col, above, below, recv, col1, col2, row1,
        up_weight, first_weight, second_weight, head_weight, biases, head_biases, land_mask,
    )

    got = lax.all_to_all(send, both, 0, 0, tiled=True)
    slots = got[:, 24, 0].astype(jnp.int32)
    ocean = pl.pallas_call(
        unpack_kernel,
        in_specs=[pl.BlockSpec(memory_space=pltpu.SMEM), pl.BlockSpec(memory_space=pltpu.VMEM)],
        out_specs=pl.BlockSpec(memory_space=pltpu.VMEM),
        out_shape=sds((CAP, 24, 128), F32),
        compiler_params=params,
        name="ocean_slots",
    )(slots, got)
    return flux, ocean.reshape(CAP, 3, 8, 128)


def solution(mesh):
    placed = (
        P(None, None, ("face", "tile"), None),
        P(None, None, ("face", "tile"), None),
        P(),
        P(),
        P(),
        P(),
        P(),
        P(),
        P(),
        P(),
        P(("face", "tile"), None),
        P(("face", "tile")),
    )
    return jax.shard_map(
        shards,
        mesh=mesh,
        in_specs=placed,
        out_specs=(P(None, None, ("face", "tile"), None), P(("face", "tile"), None, None, None)),
        check_vma=False,
    )
```

time: 881 us -> 103 us (0.12)
  waiting for transfers between devices: 417 us -> 2.22 us
  blocking collectives: 172 us -> 29.9 us
  matrix products: 110 us -> 0 us
  local copies, waits for them, and re-layouts: 63.7 us -> 1.83 us
  other arithmetic: 46.3 us -> 2.89 us
  Pallas kernels: 0 us -> 43 us
  starting transfers between devices: 47.6 us -> 21.8 us
  between operations: 14.7 us -> 0.81 us
    psum x2 -> x0, waiting for transfers between devices: 393 us -> none  [broadcast(): return lax.psum(jnp.where(mine, shard, jnp.zeros_like(shard)), axis)]
    all_gather x2 -> x0, blocking collectives: 172 us -> none  [edge_padded(): prior_column = lax.all_gather(beside_all[0], 'tile', axis=2, tiled=True)]
    dot_general x19 -> x0, matrix products: 110 us -> none  [the longest x17 87.4 us: conv_layer(): jnp.einsum('oc,bcxy->boxy', weight[row_tap, col_tap], padded[:, :, row_ta...]
    pallas_call x0 -> x4, Pallas kernels: none -> 43 us  [the longest x1 19 us: shards(): pl.pallas_call(edge_kernel, grid=(3,), in_specs=[pl.BlockSpec(memory_spac...]
    all_to_all x0 -> x1, blocking collectives: none -> 29.9 us  [shards(): got = lax.all_to_all(send, both, 0, 0, tiled=True)]
    concatenate x4 -> x0, other arithmetic: 27.2 us -> none  [the longest x2 24 us: with_halo(): block = jnp.concatenate([low, block, high], axis=dim)]
    transpose x2 -> x0, local copies, waits for them, and re-layouts: 17.6 us -> none  [the longest x1 17.6 us: shards(): jnp.einsum('aeoc,bcij->boiaje', up_weight, coarse_features, preferred_ele...]
    all_to_all x2 -> x1, starting transfers between devices: 28.1 us -> 14.8 us  [shards(): lax.all_to_all(send, both, 0, 0, axis_index_groups=groups, tiled=True)]
  transfers between devices with their start and end apart: 12 -> 6, of which waited for: 7 -> 2; matrix products, arithmetic and copies ran while one was open for 24% -> 1% of each run, Pallas kernels for 0% -> 15%
where the time goes in v1:
time: 103 us
  Pallas kernels  43 us (42%)
  blocking collectives  29.9 us (29%)
  starting transfers between devices  21.8 us (21%)
  other arithmetic  2.89 us (3%)
  waiting for transfers between devices  2.22 us (2%)
  local copies, waits for them, and re-layouts  1.83 us (2%)
    all_to_all x1, blocking collectives, shards(): got = lax.all_to_all(send, both, 0, 0, tiled=True)  29.9 us
    pallas_call x1, Pallas kernels, shards(): pl.pallas_call(edge_kernel, grid=(3,), in_specs=[pl.BlockSpec(memory_spac...  19 us
    pallas_call x1, Pallas kernels, shards(): pl.pallas_call(inner_kernel, grid=(3,), in_specs=[member((128, 8, 256)),...  14.9 us
    all_to_all x1, starting transfers between devices, shards(): lax.all_to_all(send, both, 0, 0, axis_index_groups=groups, tiled=True)  14.8 us
    pallas_call x1, Pallas kernels, shards(): pl.pallas_call(pack_kernel, grid=(3,), in_specs=[member((128, 8, 256)), m...  5.24 us
    pallas_call x1, Pallas kernels, shards(): pl.pallas_call(unpack_kernel, in_specs=[pl.BlockSpec(memory_space=pltpu.S...  3.85 us
    ppermute x1, starting transfers between devices, shards(): lax.ppermute(to_down, 'tile', [(t, t + 1) for t in range(tiles - 1)])  3.73 us
    convert_element_type x1, other arithmetic, shards(): slots = got[:, 24, 0].astype(jnp.int32)  2.88 us
  transfers between devices with their start and end apart: 6, of which 2 were waited for; matrix products, arithmetic and copies ran while one was open for 1% of the time, Pallas kernels for 15%

profile of v1, /device:TPU:0, one launch (start us, length us, event | category | flops | bytes accessed | tf_op | source)
XLA Modules:
  0.0 102.5 jit_solution(18304437461877692240)
XLA Ops:
  0.7 5.2 %pack_edges.1 = (bf16[3,3,64,512]{3,2,1,0:T(8,128)(2,1)}, bf16[3,3,64,512]{3,2,1,0:T(8,128)(2,1)}, bf16[32,96,128]{2,1,0:T(8,128)(2,1)}, bf16[96,128]{1,0:T(8,128)(2,1)}, bf16[96,128]{1,0:T(8,128)(2,1)}) custom-call(bf16[3,128,8,256]{3,2,1,0:T(8,128)(2,1)} %coarse_ref.3, bf16[3,64,16,512]{3,2,1,0:T(8,128)(2,1)} %skip_ref.3), custom_call_target="tpu_custom_call" | custom-call | tf_op jit(solution)/shard_map/pack_edges/pallas_call | solution.py:405
  5.9 0.7 collective-permute-start.3
  6.6 0.7 collective-permute-start.2
  7.2 14.8 %all-to-all-start = ((bf16[32,96,128]{2,1,0:T(8,128)(2,1)}), bf16[32,96,128]{2,1,0:T(8,128)(2,1)S(1)}, u32[]{:S(2)}, u32[]{:S(2)}) async-start(bf16[32,96,128]{2,1,0:T(8,128)(2,1)} %get-tuple-element.19), calls=%async_computation | async-start | bytes 1572864 | tf_op jit(solution)/shard_map/all_to_all | solution.py:442
  22.1 0.7 collective-permute-start.4
  22.7 3.7 %collective-permute-start = (bf16[3,3,64,512]{3,2,1,0:T(8,128)(2,1)}, bf16[3,3,64,512]{3,2,1,0:T(8,128)(2,1)S(1)}, u32[]{:S(2)}, u32[]{:S(2)}) collective-permute-start(bf16[3,3,64,512]{3,2,1,0:T(8,128)(2,1)} %get-tuple-element.17), channel_id=1, source_target_pairs={{0,1},{1,2},{2,3},{3,4},{4,5},{5,6},{6,7},{7,8},{8,9},{9,10},{10,1... | collective-permute-start | bytes 1769480 | tf_op jit(solution)/shard_map/ppermute | solution.py:428
  26.5 1.3 %collective-permute-start.1 = (bf16[3,3,64,512]{3,2,1,0:T(8,128)(2,1)}, bf16[3,3,64,512]{3,2,1,0:T(8,128)(2,1)S(1)}, u32[]{:S(2)}, u32[]{:S(2)}) collective-permute-start(bf16[3,3,64,512]{3,2,1,0:T(8,128)(2,1)} %get-tuple-element.18), channel_id=1, source_target_pairs={{1,0},{2,1},{3,2},{4,3},{5,4},{6,5},{7,6},{8,7},{9,8},{10,9},{11,1... | collective-permute-start | bytes 1769480 | tf_op jit(solution)/shard_map/ppermute | solution.py:429
  27.8 0.0 copy-done.7
  27.8 0.0 copy-done.8
  27.8 0.7 broadcast_in_dim.4.bias_ref
  28.6 14.9 %inner_rows.1 = (bf16[3,16,64,512]{3,2,1,0:T(8,128)(2,1)}, f32[3,4,64,512]{3,2,1,0:T(8,128)}, f32[3,128,128]{2,1,0:T(8,128)}, f32[3,64,128]{2,1,0:T(8,128)}) custom-call(bf16[3,128,8,256]{3,2,1,0:T(8,128)(2,1)} %coarse_ref.3, bf16[3,64,16,512]{3,2,1,0:T(8,128)(2,1)} %skip_ref.3, bf16[2,2,64,128]{3,2,1,0:T(8,128)(2,1)} %up_w_ref.3, ...), custom_call_target="tpu_custom_call" | custom-call | flops 8000000000 | bytes 9000000 | tf_op jit(solution)/shard_map/inner_rows/pallas_call | solution.py:447
  43.5 0.0 collective-permute-done.4.row1_ref
  43.5 0.0 collective-permute-done.3.col2_ref
  43.6 0.0 collective-permute-done.2.col1_ref
  43.6 0.3 collective-permute-done.above_ref
  43.9 1.9 %collective-permute-done.1.below_ref = bf16[3,3,64,512]{3,2,1,0:T(8,128)(2,1)S(1)} collective-permute-done((bf16[3,3,64,512]{3,2,1,0:T(8,128)(2,1)}, bf16[3,3,64,512]{3,2,1,0:T(8,128)(2,1)S(1)}, u32[]{:S(2)}, u32[]{:S(2)}) %collective-permute-start.1) | collective-permute-done | bytes 589856 | tf_op jit(solution)/shard_map/ppermute | solution.py:429
  45.8 0.0 all-to-all-done.recv_ref
  45.8 0.7 broadcast_in_dim.5.head_bias_ref
  46.6 0.1 copy-done.3
  46.6 0.3 copy-done.1
  46.9 19.0 %edges_and_second.1 = (f32[3,8,16,512]{3,2,1,0:T(8,128)}, bf16[128,32,128]{2,1,0:T(8,128)(2,1)}) custom-call(s32[64]{0:T(128)} %target_ref.1, bf16[3,16,64,512]{3,2,1,0:T(8,128)(2,1)} %get-tuple-element.13.first_ref, f32[3,4,64,512]{3,2,1,0:T(8,128)} %get-tuple-element.14.part_ref, f32[3,128,128]{2,1,0:T(8,128)} %get-tuple-element.15.edge_ref, ...), custom_call_target="tpu_custom_call" | custom-call | tf_op jit(solution)/shard_map/edges_and_second/pallas_call | solution.py:469
  65.9 29.9 %all_to_all.10.recv_ref = bf16[128,32,128]{2,1,0:T(8,128)(2,1)S(1)} all-to-all(bf16[128,32,128]{2,1,0:T(8,128)(2,1)} %get-tuple-element.23), channel_id=1, replica_groups=mesh['face'=4,'tile'=32] {'face','tile'}, dimensions={0} | all-to-all | bytes 2097152 | tf_op jit(solution)/shard_map/all_to_all | solution.py:507
  95.8 2.9 %fusion.slot_ref = s32[128]{0:T(128)} fusion(bf16[128,32,128]{2,1,0:T(8,128)(2,1)S(1)} %all_to_all.10.recv_ref), kind=kLoop, calls=%fused_computation.1 | loop fusion | flops 128 | bytes 768 | tf_op jit(solution)/shard_map/convert_element_type | solution.py:508
  98.7 3.8 %ocean_slots.1 = f32[44,24,128]{2,1,0:T(8,128)} custom-call(s32[128]{0:T(128)} %fusion.slot_ref, bf16[128,32,128]{2,1,0:T(8,128)(2,1)} %copy-done), custom_call_target="tpu_custom_call" | custom-call | tf_op jit(solution)/shard_map/ocean_slots/pallas_call | solution.py:509
  (19 shorter events, 0.0 us)
Async XLA Ops:
  0.6 27.2 %copy-start.7 = (f32[64]{0:T(128)S(1)}, f32[64]{0:T(128)}, u32[]{:S(2)}) copy-start(f32[64]{0:T(128)} %param.19) | copy-start | bytes 772
  0.6 27.2 %copy-start.8 = (f32[64]{0:T(128)S(1)}, f32[64]{0:T(128)}, u32[]{:S(2)}) copy-start(f32[64]{0:T(128)} %param.17) | copy-start | bytes 772
  0.7 27.2 %copy-start.9 = (f32[64]{0:T(128)S(1)}, f32[64]{0:T(128)}, u32[]{:S(2)}) copy-start(f32[64]{0:T(128)} %param.15) | copy-start | bytes 772
  5.9 37.6 %collective-permute-start.3 = (bf16[96,128]{1,0:T(8,128)(2,1)}, bf16[96,128]{1,0:T(8,128)(2,1)S(1)}, u32[]{:S(2)}, u32[]{:S(2)}) collective-permute-start(bf16[96,128]{1,0:T(8,128)(2,1)} %get-tuple-element.20), channel_id=1, source_target_pairs={{31,95},{63,127},{95,31},{127,63}} | collective-permute-start | bytes 73736 | tf_op jit(solution)/shard_map/ppermute | solution.py:437
  6.6 37.0 %collective-permute-start.2 = (bf16[96,128]{1,0:T(8,128)(2,1)}, bf16[96,128]{1,0:T(8,128)(2,1)S(1)}, u32[]{:S(2)}, u32[]{:S(2)}) collective-permute-start(bf16[96,128]{1,0:T(8,128)(2,1)} %get-tuple-element.20), channel_id=1, source_target_pairs={{31,63},{63,95},{95,127},{127,31}} | collective-permute-start | bytes 73736 | tf_op jit(solution)/shard_map/ppermute | solution.py:436
  7.2 38.6 %all-to-all-start = ((bf16[32,96,128]{2,1,0:T(8,128)(2,1)}), bf16[32,96,128]{2,1,0:T(8,128)(2,1)S(1)}, u32[]{:S(2)}, u32[]{:S(2)}) async-start(bf16[32,96,128]{2,1,0:T(8,128)(2,1)} %get-tuple-element.19), calls=%async_computation | async-start | bytes 1572864 | tf_op jit(solution)/shard_map/all_to_all | solution.py:442
  22.1 21.5 %collective-permute-start.4 = (bf16[96,128]{1,0:T(8,128)(2,1)}, bf16[96,128]{1,0:T(8,128)(2,1)S(1)}, u32[]{:S(2)}, u32[]{:S(2)}) collective-permute-start(bf16[96,128]{1,0:T(8,128)(2,1)} %get-tuple-element.21), channel_id=1, source_target_pairs={{31,127},{63,31},{95,63},{127,95}} | collective-permute-start | bytes 73736 | tf_op jit(solution)/shard_map/ppermute | solution.py:438
  22.7 21.1 %collective-permute-start = (bf16[3,3,64,512]{3,2,1,0:T(8,128)(2,1)}, bf16[3,3,64,512]{3,2,1,0:T(8,128)(2,1)S(1)}, u32[]{:S(2)}, u32[]{:S(2)}) collective-permute-start(bf16[3,3,64,512]{3,2,1,0:T(8,128)(2,1)} %get-tuple-element.17), channel_id=1, source_target_pairs={{0,1},{1,2},{2,3},{3,4},{4,5},{5,6},{6,7},{7,8},{8,9},{9,10},{10,1... | collective-permute-start | bytes 1769480 | tf_op jit(solution)/shard_map/ppermute | solution.py:428
  26.5 19.3 %collective-permute-start.1 = (bf16[3,3,64,512]{3,2,1,0:T(8,128)(2,1)}, bf16[3,3,64,512]{3,2,1,0:T(8,128)(2,1)S(1)}, u32[]{:S(2)}, u32[]{:S(2)}) collective-permute-start(bf16[3,3,64,512]{3,2,1,0:T(8,128)(2,1)} %get-tuple-element.18), channel_id=1, source_target_pairs={{1,0},{2,1},{3,2},{4,3},{5,4},{6,5},{7,6},{8,7},{9,8},{10,9},{11,1... | collective-permute-start | bytes 1769480 | tf_op jit(solution)/shard_map/ppermute | solution.py:429
  28.6 17.2 %copy-start.10 = (f32[8]{0:T(128)S(1)}, f32[8]{0:T(128)}, u32[]{:S(2)}) copy-start(f32[8]{0:T(128)} %param.21) | copy-start | bytes 100
  43.5 3.0 %copy-start.6 = (bf16[96,128]{1,0:T(8,128)(2,1)}, bf16[96,128]{1,0:T(8,128)(2,1)S(1)}, u32[]{:S(2)}) copy-start(bf16[96,128]{1,0:T(8,128)(2,1)S(1)} %collective-permute-done.4.row1_ref) | copy-start | bytes 73732
  43.6 3.0 %copy-start.4 = (bf16[96,128]{1,0:T(8,128)(2,1)}, bf16[96,128]{1,0:T(8,128)(2,1)S(1)}, u32[]{:S(2)}) copy-start(bf16[96,128]{1,0:T(8,128)(2,1)S(1)} %collective-permute-done.3.col2_ref) | copy-start | bytes 73732
  43.6 3.0 %copy-start.5 = (bf16[96,128]{1,0:T(8,128)(2,1)}, bf16[96,128]{1,0:T(8,128)(2,1)S(1)}, u32[]{:S(2)}) copy-start(bf16[96,128]{1,0:T(8,128)(2,1)S(1)} %collective-permute-done.2.col1_ref) | copy-start | bytes 73732
  43.9 2.7 %copy-start.2 = (bf16[3,3,64,512]{3,2,1,0:T(8,128)(2,1)}, bf16[3,3,64,512]{3,2,1,0:T(8,128)(2,1)S(1)}, u32[]{:S(2)}) copy-start(bf16[3,3,64,512]{3,2,1,0:T(8,128)(2,1)S(1)} %collective-permute-done.above_ref) | copy-start | bytes 1769476
  45.8 0.8 copy-start.3
  45.8 1.1 %copy-start.1 = (bf16[32,96,128]{2,1,0:T(8,128)(2,1)}, bf16[32,96,128]{2,1,0:T(8,128)(2,1)S(1)}, u32[]{:S(2)}) copy-start(bf16[32,96,128]{2,1,0:T(8,128)(2,1)S(1)} %all-to-all-done.recv_ref) | copy-start | bytes 2359300
  95.8 2.9 %copy-start = (bf16[128,32,128]{2,1,0:T(8,128)(2,1)}, bf16[128,32,128]{2,1,0:T(8,128)(2,1)S(1)}, u32[]{:S(2)}) copy-start(bf16[128,32,128]{2,1,0:T(8,128)(2,1)S(1)} %all_to_all.10.recv_ref) | copy-start | bytes 3145732

commit v2 on v0

v2 whole, which is shorter than its diff:
```python
import jax
import jax.numpy as jnp
from jax import lax
from jax.experimental import pallas as pl
from jax.experimental.pallas import tpu as pltpu
from jax.sharding import PartitionSpec as P

BF = jnp.bfloat16
F32 = jnp.float32
ROWS = 16
COLS = 512
BLOCK = 128
CAP = 44
VMEM_LIMIT = 58 * 1024 * 1024
UNPACK_LIMIT = 16 * 1024 * 1024


def dot(a, b):
    return jnp.dot(a, b, preferred_element_type=F32)


def silu(v):
    half = 0.5 * v
    return half * jnp.tanh(half) + half


def lanes_of(shape):
    return lax.broadcasted_iota(jnp.int32, shape, len(shape) - 1)


def wide(column, tiles):
    return jnp.concatenate([column] * tiles, axis=1)


def taps(row):
    lane = lanes_of(row.shape)
    zero = jnp.zeros_like(row)
    before = jnp.where(lane == 0, zero, pltpu.roll(row, 1, 1))
    after = jnp.where(lane == COLS - 1, zero, pltpu.roll(row, COLS - 1, 1))
    return jnp.concatenate([before, row, after], axis=0)


def spread(coarse):
    lane = lanes_of((128, 128))
    parts = [
        jnp.take_along_axis(coarse[:, 128 * p : 128 * p + 128], lane // 2 + 64 * h, axis=1)
        for p in range(2)
        for h in range(2)
    ]
    even = lane % 2 == 0
    zero = jnp.zeros((128, 128), F32)
    top = jnp.concatenate([jnp.where(even, part, zero) for part in parts], axis=1)
    low = jnp.concatenate([jnp.where(even, zero, part) for part in parts], axis=1)
    return jnp.concatenate([top, low], axis=0).astype(BF)


def up_rows(up_ref):
    return jnp.concatenate(
        [jnp.concatenate([up_ref[a, 0], up_ref[a, 1]], axis=1) for a in range(2)], axis=0
    )


def row_taps(weight_ref, r):
    return jnp.concatenate([weight_ref[r, s] for s in range(3)], axis=1)


def turned_taps(weight_ref, r):
    return jnp.concatenate([weight_ref[s, 2 - r] for s in range(3)], axis=1)


def bias_column(row_ref, height):
    return jnp.broadcast_to(row_ref[...], (128, height)).T


def begin(copies):
    for copy in copies:
        copy.start()


def finish(copies):
    for copy in copies:
        copy.wait()


def pack_kernel(
    coarse_hbm, skip_hbm, one_hbm, two_hbm, send_hbm, col_ref, edge_ref,
    coarse_ref, skip_ref, one_ref, two_ref, send_ref, skip_t, coarse_t, sems,
):
    tile = lax.axis_index("tile")
    bottom = tile == lax.axis_size("tile") - 1
    even = lax.rem(tile, 2) == 0

    def loads(member):
        return [
            pltpu.make_async_copy(skip_hbm.at[member], skip_ref.at[member], sems.at[0, member]),
            pltpu.make_async_copy(coarse_hbm.at[member], coarse_ref.at[member], sems.at[1, member]),
        ]

    def store_one(member):
        return [pltpu.make_async_copy(one_ref.at[member], one_hbm.at[member], sems.at[2, member])]

    for member in range(3):
        begin(loads(member))

    def one(member, carry):
        finish(loads(member))
        pack_member(
            member, bottom, even, coarse_ref, skip_ref, one_ref, two_ref, send_ref, col_ref, edge_ref, skip_t, coarse_t
        )

        begin(store_one(member))
        return carry

    lax.fori_loop(0, 3, one, 0)

    @pl.when(bottom)
    def _():
        two_ref[:, 0, :, :128] = edge_ref[...].reshape(3, 64, 128)

    store_two = pltpu.make_async_copy(two_ref, two_hbm, sems.at[3, 0])
    store_two.start()
    ends = pltpu.make_async_copy(send_ref.at[31], send_hbm.at[31], sems.at[4, 0])
    rest = pltpu.make_async_copy(send_ref.at[pl.ds(0, 31)], send_hbm.at[pl.ds(0, 31)], sems.at[4, 1])
    ends.start()

    @pl.when(bottom)
    def _():
        rest.start()

    for member in range(3):
        finish(store_one(member))
    store_two.wait()
    ends.wait()

    @pl.when(bottom)
    def _():
        rest.wait()


def pack_member(
    member, bottom, even, coarse_ref, skip_ref, one_ref, two_ref, send_ref, col_ref, edge_ref, skip_t, coarse_t
):
    own = pl.ds(pl.multiple_of(member * 32, 32), 32)
    rows = jnp.swapaxes(skip_ref[member], 0, 1)
    coarse_rows = jnp.swapaxes(coarse_ref[member], 0, 1)

    def pair(row):
        return jnp.concatenate([row[:64], row[64:]], axis=1)

    top = (rows[0], rows[1], pair(coarse_rows[0]))
    low = (rows[14], rows[15], pair(coarse_rows[7]))
    for k in range(3):
        one_ref[member, k] = jnp.where(even, low[k], top[k])
        two_ref[member, k] = jnp.where(even, top[k], low[k])

    lane = lanes_of((128, 128))
    skip_cols = jnp.zeros((128, 128), F32)
    coarse_cols = jnp.zeros((128, 128), F32)
    for x in range(ROWS):
        end = rows[x][:, 384:512].astype(F32)
        both = jnp.concatenate([pltpu.roll(end, x + 1, 1), pltpu.roll(end, x + 2, 1)], axis=0)
        skip_cols = jnp.where(lane == x, both, skip_cols)
    for i in range(ROWS // 2):
        end = coarse_rows[i][:, 128:256].astype(F32)
        coarse_cols = jnp.where(lane == i, pltpu.roll(end, i + 1, 1), coarse_cols)
    piece = jnp.concatenate([skip_cols.T[:16], coarse_cols.T[:16]], axis=0).astype(BF)
    col_ref[own, :] = piece
    edge_ref[own, :] = piece
    send_ref[31, own, :] = piece

    @pl.when(bottom)
    def _():
        skip_t[...] = jnp.zeros_like(skip_t)
        coarse_t[...] = jnp.zeros_like(coarse_t)
        both = jnp.concatenate([rows[15], rows[14]], axis=0).astype(F32)
        for q in range(4):
            skip_t[8 + 128 * q : 136 + 128 * q, :] = both[:, 128 * q : 128 * q + 128].T
        below = coarse_rows[7].astype(F32)
        for q in range(2):
            coarse_t[8 + 128 * q : 136 + 128 * q, :] = below[:, 128 * q : 128 * q + 128].T
        for j in range(32):
            part = jnp.concatenate(
                [
                    skip_t[16 * j + 6 : 16 * j + 26, :],
                    coarse_t[8 * j + 7 : 8 * j + 19, :],
                ],
                axis=0,
            ).astype(BF)
            if j < 31:
                send_ref[j, own, :] = part
            else:
                edge_ref[pl.ds(pl.multiple_of(96 + member * 32, 32), 32), :] = part


def inner_kernel(
    coarse_hbm, skip_hbm, up_w_hbm, w_hbm, up_bias_hbm, first_bias_hbm, first_hbm, part_hbm, cols_hbm,
    coarse_ref, skip_ref, up_w_ref, w_ref, up_bias_ref, first_bias_ref, first_ref, part_ref, cols_ref, rows_ref, sems,
):
    bottom = lax.axis_index("tile") == lax.axis_size("tile") - 1

    def loads(member):
        return [
            pltpu.make_async_copy(skip_hbm.at[member], skip_ref.at[member], sems.at[0, member]),
            pltpu.make_async_copy(coarse_hbm.at[member], coarse_ref.at[member], sems.at[1, member]),
        ]

    def stores(member):
        return [
            pltpu.make_async_copy(first_ref.at[member], first_hbm.at[member], sems.at[2, member]),
            pltpu.make_async_copy(part_ref.at[member], part_hbm.at[member], sems.at[3, member]),
        ]

    small = [
        pltpu.make_async_copy(source, target, sems.at[5, k])
        for k, (source, target) in enumerate(
            [
                (up_w_hbm, up_w_ref),
                (w_hbm, w_ref),
                (up_bias_hbm, up_bias_ref),
                (first_bias_hbm, first_bias_ref),
            ]
        )
    ]
    begin(small)
    begin(loads(0))
    finish(small)
    up_w = up_rows(up_w_ref)
    up_bias = wide(bias_column(up_bias_ref, 64), 4)
    first_bias = wide(bias_column(first_bias_ref, 64), 4)
    by_row = [row_taps(w_ref, r) for r in range(3)]
    weight = jnp.concatenate(by_row, axis=0)
    turned = jnp.where(bottom, turned_taps(w_ref, 0), by_row[0])
    last_weight = jnp.concatenate([turned, by_row[1], by_row[2]], axis=0)
    cols_ref[...] = jnp.zeros_like(cols_ref)

    def one(member, carry):
        finish(loads(member))

        @pl.when(member < 2)
        def _():
            begin(loads(member + 1))

        rows = jnp.swapaxes(skip_ref[member], 0, 1)
        coarse_rows = jnp.swapaxes(coarse_ref[member], 0, 1)
        lane = lanes_of((128, 128))
        lane64 = lanes_of((64, 128))
        ends = jnp.zeros((128, 128), F32)
        last = jnp.zeros((64, 128), F32)
        before = [None, None]
        for k in range(ROWS // 2):
            fine = dot(up_w, spread(coarse_rows[k].astype(F32)))
            for a in range(2):
                i = 2 * k + a
                upsampled = (fine[64 * a : 64 * a + 64] + up_bias).astype(BF)
                row = jnp.concatenate([upsampled, rows[i]], axis=0)
                rows_ref[i] = row
                end = row[:, 384:512].astype(F32)
                ends = jnp.where(lane == i + 2, pltpu.roll(end, i + 3, 1), ends)
        for k in range(ROWS // 2):
            for a in range(2):
                i = 2 * k + a
                row = rows_ref[i]
                summed = dot(last_weight if i == ROWS - 1 else weight, taps(row))
                low, mid, high = summed[:64], summed[64:128], summed[128:]
                done = high if before[0] is None else before[0] + high
                before = [mid if before[1] is None else before[1] + mid, low]
                if i == 0:
                    part_ref[member, 0] = done
                elif i == 1:
                    part_ref[member, 1] = done
                else:
                    value = done + first_bias
                    first_ref[member, i - 1] = silu(value).astype(BF)
                    last = jnp.where(lane64 == i + 1, pltpu.roll(value[:, 384:512], i + 2, 1), last)
        part_ref[member, 2] = before[0]
        part_ref[member, 3] = before[1]
        shift = member * 32
        cols_ref[:128] = cols_ref[:128] + pltpu.roll(ends, shift, 1)
        cols_ref[128:] = cols_ref[128:] + pltpu.roll(last, shift, 1)
        begin(stores(member))
        return carry

    lax.fori_loop(0, 3, one, 0)
    cols = pltpu.make_async_copy(cols_ref, cols_hbm, sems.at[4, 0])
    cols.start()
    for member in range(3):
        finish(stores(member))
    cols.wait()


def edge_kernel(
    first_hbm, part_hbm, cols_hbm, one_ref, two_ref, recv_ref, far_ref, across_ref,
    up_w_hbm, w1_hbm, w2_hbm, head_hbm, up_bias_hbm, first_bias_hbm, second_bias_hbm, head_bias_hbm, mask_hbm,
    target_hbm, flux_ref, send_ref,
    first_ref, part_ref, cols_ref, up_w_ref, w1_ref, w2_ref, head_ref, up_bias_ref, first_bias_ref,
    second_bias_ref, head_bias_ref, mask_ref, target_ref, halo_skip, halo_coarse, piece_ref, rows_ref, second_ref, sems,
):
    tile = lax.axis_index("tile")
    bottom = tile == lax.axis_size("tile") - 1
    top = tile == 0
    even_tile = lax.rem(tile, 2) == 0
    even_face = lax.rem(lax.axis_index("face"), 2) == 0

    def loads(member):
        return [
            pltpu.make_async_copy(first_hbm.at[member], first_ref.at[member], sems.at[0, member]),
            pltpu.make_async_copy(part_hbm.at[member], part_ref.at[member], sems.at[1, member]),
        ]

    small = [
        pltpu.make_async_copy(source, target, sems.at[2, k])
        for k, (source, target) in enumerate(
            [
                (up_w_hbm, up_w_ref),
                (w1_hbm, w1_ref),
                (w2_hbm, w2_ref),
                (head_hbm, head_ref),
                (up_bias_hbm, up_bias_ref),
                (first_bias_hbm, first_bias_ref),
                (second_bias_hbm, second_bias_ref),
                (head_bias_hbm, head_bias_ref),
                (mask_hbm, mask_ref),
                (target_hbm, target_ref),
                (cols_hbm, cols_ref),
            ]
        )
    ]
    begin(small)
    for member in range(3):
        begin(loads(member))

    @pl.when(jnp.logical_not(bottom))
    def _():
        for member in range(3):
            for a in range(2):
                halo_skip[member, a] = jnp.where(even_tile, one_ref[member, a], two_ref[member, a])
            both = jnp.where(even_tile, one_ref[member, 2], two_ref[member, 2]).astype(F32)
            halo_coarse[member] = jnp.concatenate([both[:, :256], both[:, 256:]], axis=0)
        piece_ref[...] = recv_ref[31].astype(F32)

    @pl.when(bottom)
    def _():
        near, far = two_ref[:, 0, :, :128].reshape(192, 128), far_ref[...]
        from_previous = jnp.where(even_face, far[:96], near[:96])
        for member in range(3):
            own = slice(32 * member, 32 * member + 32)
            pieces = [recv_ref[j].astype(F32)[own] for j in range(31)]
            pieces.append(from_previous.astype(F32)[own])
            for q in range(4):
                stacked = jnp.concatenate([pieces[8 * q + j][:16] for j in range(8)], axis=0).T.astype(BF)
                halo_skip[member, 0, :, 128 * q : 128 * q + 128] = stacked[:64]
                halo_skip[member, 1, :, 128 * q : 128 * q + 128] = stacked[64:]
            for q in range(2):
                stacked = jnp.concatenate([pieces[16 * q + j][16:24] for j in range(16)], axis=0).T
                halo_coarse[member, :, 128 * q : 128 * q + 128] = stacked
        piece_ref[...] = jnp.where(even_face, near[96:], far[96:]).astype(F32)

    finish(small)
    up_bias = bias_column(up_bias_ref, 64)
    up_bias_wide = wide(up_bias, 4)
    first_bias = bias_column(first_bias_ref, 64)
    first_bias_wide = wide(first_bias, 4)
    second_bias_wide = wide(bias_column(second_bias_ref, 64), 4)
    head_bias = wide(bias_column(head_bias_ref, 8), 4)
    lane = lanes_of((128, 128))
    place = lax.rem(lane, 32)
    lane64 = lanes_of((64, 128))
    place64 = lax.rem(lane64, 32)
    zero = jnp.zeros((128, 128), F32)
    ghost_rows = jnp.zeros((32, 128), F32)

    up_w = up_rows(up_w_ref)
    turned_up = jnp.concatenate(
        [jnp.concatenate([up_w_ref[0, 1 - q], up_w_ref[1, 1 - q]], axis=1) for q in range(2)], axis=0
    )
    below_w = jnp.where(bottom, turned_up, up_w)
    edge = cols_ref[:128]
    for member in range(3):
        both = jnp.where(even_tile, two_ref[member, 2], one_ref[member, 2]).astype(F32)
        fine = dot(up_w, spread(jnp.concatenate([both[:, :256], both[:, 256:]], axis=0)))
        fine_below = dot(below_w, spread(halo_coarse[member]))
        for a in range(2):
            upsampled = (fine[64 * a : 64 * a + 64] + up_bias_wide).astype(BF)
            skip = jnp.where(even_tile, two_ref[member, a], one_ref[member, a])
            row = jnp.concatenate([upsampled, skip], axis=0)
            row = jnp.where(top, jnp.zeros_like(row), row)
            upsampled = (fine_below[64 * a : 64 * a + 64] + up_bias_wide).astype(BF)
            row_below = jnp.concatenate([upsampled, halo_skip[member, a]], axis=0)
            for x, value in ((a, row), (18 + a, row_below)):
                rows_ref[member, a if x < 2 else 2 + a] = value
                end = pltpu.roll(value[:, 384:512].astype(F32), (32 * member + x + 1) % 128, 1)
                edge = jnp.where(lane == 32 * member + x, end, edge)

    pixel = tile * ROWS - 2 + place
    piece = jnp.concatenate([piece_ref[...], ghost_rows], axis=0).T
    doubled = jnp.take_along_axis(piece, jnp.minimum(lane - place + 20 + lax.div(place, 2), 127), axis=1)
    even = lax.rem(lane, 2) == 0
    spread_piece = jnp.concatenate(
        [jnp.where(even, doubled, zero), jnp.where(even, zero, doubled)], axis=0
    ).astype(BF)
    ghost_up = jnp.concatenate(
        [jnp.concatenate([up_w_ref[1 - q, 0], up_w_ref[1 - q, 1]], axis=1) for q in range(2)], axis=0
    )
    ghost_fine = dot(ghost_up, spread_piece)
    inside = (place < 20) & (pixel >= 0) & (pixel < COLS) & (lane < 96)
    ghost = []
    for q in range(2):
        upsampled = (ghost_fine[64 * q : 64 * q + 64] + up_bias).astype(BF).astype(F32)
        joined = jnp.concatenate([upsampled, piece[64 * q : 64 * q + 64]], axis=0)
        ghost.append(jnp.where(inside, joined, zero))

    corner = jnp.concatenate([across_ref[...].astype(F32), ghost_rows], axis=0).T
    at_corner = dot(
        jnp.concatenate([up_w_ref[1, 1], up_w_ref[1, 0], up_w_ref[0, 1]], axis=0), corner.astype(BF)
    )
    held = (place == 18) & bottom & (lane < 96)

    def corner_column(k, q, x):
        upsampled = (at_corner[64 * k : 64 * k + 64] + up_bias).astype(BF).astype(F32)
        joined = jnp.concatenate(
            [pltpu.roll(upsampled, 123, 1), pltpu.roll(corner[64 * q : 64 * q + 64], 18 - x, 1)], axis=0
        )
        return jnp.where(held, joined, zero)

    corner0 = corner_column(0, 0, 15)
    corner1 = corner_column(1, 1, 15)
    corner2 = corner_column(2, 0, 14)

    def around(joined):
        return [pltpu.roll(joined, 1, 1), joined, pltpu.roll(joined, 127, 1)]

    weight = jnp.concatenate([w1_ref[r, 2] for r in range(3)], axis=1)
    added = dot(weight, jnp.concatenate(around(ghost[0].astype(BF)), axis=0))
    weight = jnp.concatenate([w1_ref[2, 1], w1_ref[2, 0]], axis=1)
    added_bottom = dot(weight, jnp.concatenate([corner0, corner2], axis=0).astype(BF))
    added = jnp.where((place64 == 18) & bottom, added_bottom, added)

    edge = jnp.where((place == 18) & bottom, zero, edge)
    columns = [edge.astype(BF), (ghost[0] + corner0).astype(BF), (ghost[1] + corner1).astype(BF)]
    weight = jnp.concatenate([w1_ref[2 - s, r] for s in range(3) for r in range(3)], axis=1)
    summed = dot(weight, jnp.concatenate([part for joined in columns for part in around(joined)], axis=0))
    pixel64 = tile * ROWS - 2 + place64
    inside64 = (place64 >= 1) & (place64 <= 18) & (pixel64 >= 0) & (pixel64 < COLS)
    first_ghost = jnp.where(inside64, silu(summed + first_bias), jnp.zeros((64, 128), F32))
    last = silu(cols_ref[128:] + added)

    by_row = [row_taps(w1_ref, r) for r in range(3)]
    turned = [jnp.where(bottom, turned_taps(w1_ref, r), by_row[r]) for r in range(3)]
    second_weight = jnp.concatenate([row_taps(w2_ref, r) for r in range(3)], axis=0)
    head = head_ref[...]
    lane512 = lanes_of((64, COLS))

    def one(member, carry):
        base = 125 - 32 * member

        def finished(summed, x):
            end = summed[:, 384:512] + jnp.where(lane64 == 127, pltpu.roll(added, base - x, 1), 0.0)
            summed = jnp.concatenate([summed[:, :384], end], axis=1)
            return silu(summed + first_bias_wide).astype(BF)

        finish(loads(member))
        term = dot(by_row[0], taps(rows_ref[member, 0]))
        terms = dot(jnp.concatenate([by_row[1], by_row[0]], axis=0), taps(rows_ref[member, 1]))
        row_m1 = finished(part_ref[member, 0] + term + terms[:64], -1)
        row_0 = finished(part_ref[member, 1] + terms[64:], 0)
        term = dot(turned[2], taps(rows_ref[member, 3]))
        terms = dot(jnp.concatenate([turned[1], by_row[2]], axis=0), taps(rows_ref[member, 2]))
        row_15 = finished(part_ref[member, 2] + terms[64:], 15)
        row_16 = finished(part_ref[member, 3] + term + terms[:64], 16)
        outer = {-1: jnp.where(top, jnp.zeros_like(row_m1), row_m1), 0: row_0, 15: row_15, 16: row_16}

        before = [None, None]
        for x in range(-1, ROWS + 1):
            if x in outer:
                row = outer[x]
            else:
                row = first_ref[member, x]
                end = jnp.where(lane64 == 127, pltpu.roll(last, base - x, 1).astype(BF), row[:, 384:512])
                row = jnp.concatenate([row[:, :384], end], axis=1)
            moved = pltpu.roll(row, COLS - 1, 1)
            end = jnp.where(
                lane64 == 127, pltpu.roll(first_ghost, base - x, 1).astype(BF), moved[:, 384:512]
            )
            after = jnp.concatenate([moved[:, :384], end], axis=1)
            first_part = jnp.where(lane512 == 0, jnp.zeros_like(row), pltpu.roll(row, 1, 1))
            summed = dot(second_weight, jnp.concatenate([first_part, row, after], axis=0))
            low, mid, high = summed[:64], summed[64:128], summed[128:]
            done = high if before[0] is None else before[0] + high
            before = [mid if before[1] is None else before[1] + mid, low]
            n = x - 1
            if n >= 0:
                second_ref[n] = silu(done + second_bias_wide).astype(BF)
        for n in range(ROWS):
            flux_ref[member, :, n, :] = dot(head, second_ref[n]) + head_bias
        return carry

    lax.fori_loop(0, 3, one, 0)

    target = target_ref[...]
    owner = jnp.where(target >= 0, lax.div(jnp.maximum(target, 0), CAP), -1)
    slot = jnp.where(target >= 0, target - owner * CAP + 1, 0)
    wanted = lax.broadcasted_iota(jnp.int32, (128, 64), 0)
    by_pixel_row = jnp.where(jnp.broadcast_to(owner, (128, 64)) == wanted, 1.0, 0.0).astype(BF)
    block = lax.broadcasted_iota(jnp.int32, (64, 64), 0)
    place = lax.broadcasted_iota(jnp.int32, (64, 64), 1)
    moved = jnp.where(block == 4 * lax.rem(place, 16) + lax.div(place, 16), 1.0, 0.0).astype(BF)
    chosen = dot(by_pixel_row, moved).astype(BF)
    mask = mask_ref[...].astype(F32)
    packed = []
    for member in range(3):
        for k in range(8):
            masked = (flux_ref[member, k] * mask).astype(BF)
            blocks = jnp.concatenate([masked[:, 128 * q : 128 * q + 128] for q in range(4)], axis=0)
            packed.append(dot(chosen, blocks).astype(BF))
    slots = jnp.broadcast_to(slot.astype(F32), (128, 64)).astype(BF)
    slots = jnp.sum(by_pixel_row.astype(F32) * slots.astype(F32), axis=1, keepdims=True)
    slots = jnp.broadcast_to(slots, (128, 128)).astype(BF)
    packed += [slots] * 8
    send_ref[...] = jnp.swapaxes(jnp.stack(packed, axis=0), 0, 1)


def unpack_kernel(recv_ref, out_ref):
    rows = jnp.swapaxes(recv_ref[...], 0, 1)
    slots = rows[24].astype(F32).T[:48]
    wanted = (lax.broadcasted_iota(jnp.int32, slots.shape, 0) + 1).astype(F32)
    chosen = jnp.where(slots == wanted, 1.0, 0.0).astype(BF)
    for k in range(24):
        out_ref[:, k, :] = dot(chosen, rows[k])[:CAP]


def vmem(count):
    return [pl.BlockSpec(memory_space=pltpu.VMEM)] * count


def hbm(count):
    return [pl.BlockSpec(memory_space=pltpu.HBM)] * count


def shards(
    coarse_features,
    skip_features,
    up_weight,
    up_bias,
    first_weight,
    first_bias,
    second_weight,
    second_bias,
    head_weight,
    head_bias,
    land_mask,
    block_target,
):
    faces = lax.axis_size("face")
    tiles = lax.axis_size("tile")
    devices = faces * tiles
    params = pltpu.CompilerParams(vmem_limit_bytes=VMEM_LIMIT)
    sds = jax.ShapeDtypeStruct

    one, two, send, col, edges = pl.pallas_call(
        pack_kernel,
        in_specs=hbm(2),
        out_specs=hbm(3) + vmem(2),
        out_shape=[
            sds((3, 3, 64, 512), BF),
            sds((3, 3, 64, 512), BF),
            sds((32, 96, 128), BF),
            sds((96, 128), BF),
            sds((192, 128), BF),
        ],
        scratch_shapes=[
            pltpu.VMEM((3, 128, 8, 256), BF),
            pltpu.VMEM((3, 64, 16, 512), BF),
            pltpu.VMEM((3, 3, 64, 512), BF),
            pltpu.VMEM((3, 3, 64, 512), BF),
            pltpu.VMEM((32, 96, 128), BF),
            pltpu.VMEM((544, 128), F32),
            pltpu.VMEM((272, 128), F32),
            pltpu.SemaphoreType.DMA((5, 3)),
        ],
        compiler_params=params,
        name="pack_edges",
    )(coarse_features, skip_features)

    last = tiles - 1

    both = ("face", "tile")

    def swapped(bits):
        return [(f * tiles + last, (f ^ bits) * tiles + last) for f in range(faces)]

    strips = [f * tiles for f in range(faces)]
    first_pairs = [(s + t, s + (t ^ 1)) for s in strips for t in range(tiles)]
    second_pairs = [(s + t, s + ((t - 1) ^ 1) + 1) for s in strips for t in range(1, last)]
    got_one = lax.ppermute(one, both, first_pairs)
    got_two = lax.ppermute(two, both, second_pairs + swapped(1))
    far = lax.ppermute(edges, both, swapped(3))
    across = lax.ppermute(col, both, swapped(2))
    groups = [
        [f * tiles + t for t in range(last)] + [((f + 1) % faces) * tiles + last] for f in range(faces)
    ]
    recv = lax.all_to_all(send, both, 0, 0, axis_index_groups=groups, tiled=True)

    up_bias, first_bias, second_bias = (b.reshape(1, 64) for b in (up_bias, first_bias, second_bias))
    first, parts, cols = pl.pallas_call(
        inner_kernel,
        in_specs=hbm(6),
        out_specs=hbm(3),
        out_shape=[sds((3, 16, 64, 512), BF), sds((3, 4, 64, 512), F32), sds((192, 128), F32)],
        scratch_shapes=[
            pltpu.VMEM((3, 128, 8, 256), BF),
            pltpu.VMEM((3, 64, 16, 512), BF),
            pltpu.VMEM((2, 2, 64, 128), BF),
            pltpu.VMEM((3, 3, 64, 128), BF),
            pltpu.VMEM((1, 64), F32),
            pltpu.VMEM((1, 64), F32),
            pltpu.VMEM((3, 16, 64, 512), BF),
            pltpu.VMEM((3, 4, 64, 512), F32),
            pltpu.VMEM((192, 128), F32),
            pltpu.VMEM((16, 128, 512), BF),
            pltpu.SemaphoreType.DMA((6, 4)),
        ],
        compiler_params=params,
        name="inner_rows",
    )(coarse_features, skip_features, up_weight, first_weight, up_bias, first_bias)

    flux, send = pl.pallas_call(
        edge_kernel,
        in_specs=hbm(3) + vmem(5) + hbm(10),
        out_specs=vmem(2),
        out_shape=[sds((3, 8, 16, 512), F32), sds((devices, 32, 128), BF)],
        scratch_shapes=[
            pltpu.VMEM((3, 16, 64, 512), BF),
            pltpu.VMEM((3, 4, 64, 512), F32),
            pltpu.VMEM((192, 128), F32),
            pltpu.VMEM((2, 2, 64, 128), BF),
            pltpu.VMEM((3, 3, 64, 128), BF),
            pltpu.VMEM((3, 3, 64, 64), BF),
            pltpu.VMEM((8, 64), BF),
            pltpu.VMEM((1, 64), F32),
            pltpu.VMEM((1, 64), F32),
            pltpu.VMEM((1, 64), F32),
            pltpu.VMEM((1, 8), F32),
            pltpu.VMEM((16, 512), jnp.int32),
            pltpu.VMEM((1, 64), jnp.int32),
            pltpu.VMEM((3, 2, 64, 512), BF),
            pltpu.VMEM((3, 128, 256), F32),
            pltpu.VMEM((96, 128), F32),
            pltpu.VMEM((3, 4, 128, 512), BF),
            pltpu.VMEM((16, 64, 512), BF),
            pltpu.SemaphoreType.DMA((3, 11)),
        ],
        compiler_params=params,
        name="edges_and_second",
    )(
        first, parts, cols, got_one, got_two, recv, far, across,
        up_weight, first_weight, second_weight, head_weight, up_bias, first_bias, second_bias,
        head_bias.reshape(1, 8), land_mask, block_target.reshape(1, 64),
    )

    got = lax.all_to_all(send, both, 0, 0, tiled=True)
    ocean = pl.pallas_call(
        unpack_kernel,
        in_specs=vmem(1),
        out_specs=vmem(1)[0],
        out_shape=sds((CAP, 24, 128), F32),
        compiler_params=pltpu.CompilerParams(vmem_limit_bytes=UNPACK_LIMIT),
        name="ocean_slots",
    )(got)
    return flux, ocean.reshape(CAP, 3, 8, 128)


def solution(mesh):
    placed = (
        P(None, None, ("face", "tile"), None),
        P(None, None, ("face", "tile"), None),
        P(),
        P(),
        P(),
        P(),
        P(),
        P(),
        P(),
        P(),
        P(("face", "tile"), None),
        P(("face", "tile")),
    )
    return jax.shard_map(
        shards,
        mesh=mesh,
        in_specs=placed,
        out_specs=(P(None, None, ("face", "tile"), None), P(("face", "tile"), None, None, None)),
        check_vma=False,
    )
```

time: 881 us -> 82.9 us (0.09); the launches traced: 872 us -> 82.5 us
  waiting for transfers between devices: 417 us -> 8.76 us
  blocking collectives: 172 us -> 29.3 us
  matrix products: 110 us -> 0 us
  local copies, waits for them, and re-layouts: 63.7 us -> 1.23 us
  other arithmetic: 46.3 us -> 0 us
  starting transfers between devices: 47.6 us -> 13.2 us
  Pallas kernels: 0 us -> 29.3 us
  between operations: 14.7 us -> 0.75 us
    psum x2 -> x0, waiting for transfers between devices: 393 us -> none  [broadcast(): return lax.psum(jnp.where(mine, shard, jnp.zeros_like(shard)), axis)]
    all_gather x2 -> x0, blocking collectives: 172 us -> none  [edge_padded(): prior_column = lax.all_gather(beside_all[0], 'tile', axis=2, tiled=True)]
    dot_general x19 -> x0, matrix products: 110 us -> none  [the longest x17 87.4 us: conv_layer(): jnp.einsum('oc,bcxy->boxy', weight[row_tap, col_tap], padded[:, :, row_ta...]
    all_to_all x0 -> x1, blocking collectives: none -> 29.3 us  [shards(): got = lax.all_to_all(send, both, 0, 0, tiled=True)]
    pallas_call x0 -> x4, Pallas kernels: none -> 29.3 us  [the longest x1 12.2 us: shards(): pl.pallas_call(edge_kernel, in_specs=hbm(3) + vmem(5) + hbm(10), out_spec...]
    concatenate x4 -> x0, other arithmetic: 27.2 us -> none  [the longest x2 24 us: with_halo(): block = jnp.concatenate([low, block, high], axis=dim)]
    all_to_all x2 -> x1, starting transfers between devices: 28.1 us -> 9.27 us  [shards(): lax.all_to_all(send, both, 0, 0, axis_index_groups=groups, tiled=True)]
    transpose x2 -> x0, local copies, waits for them, and re-layouts: 17.6 us -> none  [the longest x1 17.6 us: shards(): jnp.einsum('aeoc,bcij->boiaje', up_weight, coarse_features, preferred_ele...]
  transfers between devices with their start and end apart: 12 -> 5, of which waited for: 7 -> 1; matrix products, arithmetic and copies ran while one was open for 24% -> 0% of each run, Pallas kernels for 0% -> 13%
where the time goes in v2:
time: 82.9 us; the launch traced here: 82.5 us
  Pallas kernels  29.3 us (35%)
  blocking collectives  29.3 us (35%)
  starting transfers between devices  13.2 us (16%)
  waiting for transfers between devices  8.76 us (11%)
  local copies, waits for them, and re-layouts  1.23 us (1%)
    all_to_all x1, blocking collectives, shards(): got = lax.all_to_all(send, both, 0, 0, tiled=True)  29.3 us
    pallas_call x1, Pallas kernels, shards(): pl.pallas_call(edge_kernel, in_specs=hbm(3) + vmem(5) + hbm(10), out_spec...  12.2 us
    pallas_call x1, Pallas kernels, shards(): pl.pallas_call(inner_kernel, in_specs=hbm(6), out_specs=hbm(3), out_shape...  10.8 us
    all_to_all x1, starting transfers between devices, shards(): lax.all_to_all(send, both, 0, 0, axis_index_groups=groups, tiled=True)  9.27 us
    ppermute x1, waiting for transfers between devices, shards(): got_one = lax.ppermute(one, both, first_pairs)  8.75 us
    pallas_call x1, Pallas kernels, shards(): pl.pallas_call(pack_kernel, in_specs=hbm(2), out_specs=hbm(3) + vmem(2),...  4.79 us
    ppermute x1, starting transfers between devices, shards(): got_one = lax.ppermute(one, both, first_pairs)  1.87 us
  transfers between devices with their start and end apart: 5, of which 1 were waited for; matrix products, arithmetic and copies ran while one was open for 0% of the time, Pallas kernels for 13%

profile of v2, /device:TPU:0, one launch (start us, length us, event | category | flops | bytes accessed | tf_op | source)
XLA Modules:
  0.0 82.5 jit_solution(13092988939876618495)
XLA Ops:
  0.6 4.8 %pack_edges.1 = (bf16[3,3,64,512]{3,2,1,0:T(8,128)(2,1)}, bf16[3,3,64,512]{3,2,1,0:T(8,128)(2,1)}, bf16[32,96,128]{2,1,0:T(8,128)(2,1)}, bf16[96,128]{1,0:T(8,128)(2,1)}, bf16[192,128]{1,0:T(8,128)(2,1)}) custom-call(bf16[3,128,8,256]{3,2,1,0:T(8,128)(2,1)} %coarse_hbm.3, bf16[3,64,16,512]{3,2,1,0:T(8,128)(2,1)} %skip_hbm.3), custom_call_target="tpu_custom_call" | custom-call | tf_op jit(solution)/shard_map/pack_edges/pallas_call | solution.py:559
  5.4 9.3 %all-to-all-start = ((bf16[32,96,128]{2,1,0:T(8,128)(2,1)}), bf16[32,96,128]{2,1,0:T(8,128)(2,1)S(1)}, u32[]{:S(2)}, u32[]{:S(2)}) async-start(bf16[32,96,128]{2,1,0:T(8,128)(2,1)} %get-tuple-element.17), calls=%async_computation | async-start | bytes 1572864 | tf_op jit(solution)/shard_map/all_to_all | solution.py:601
  14.7 1.9 %collective-permute-start = (bf16[3,3,64,512]{3,2,1,0:T(8,128)(2,1)}, bf16[3,3,64,512]{3,2,1,0:T(8,128)(2,1)S(1)}, u32[]{:S(2)}, u32[]{:S(2)}) collective-permute-start(bf16[3,3,64,512]{3,2,1,0:T(8,128)(2,1)} %get-tuple-element.15), channel_id=1, source_target_pairs={{0,1},{1,0},{2,3},{3,2},{4,5},{5,4},{6,7},{7,6},{8,9},{9,8},{10,11... | collective-permute-start | bytes 1769480 | tf_op jit(solution)/shard_map/ppermute | solution.py:594
  16.6 0.7 collective-permute-start.1
  17.3 0.7 collective-permute-start.2
  17.9 0.7 collective-permute-start.3
  18.6 10.8 %inner_rows.1 = (bf16[3,16,64,512]{3,2,1,0:T(8,128)(2,1)}, f32[3,4,64,512]{3,2,1,0:T(8,128)}, f32[192,128]{1,0:T(8,128)}) custom-call(bf16[3,128,8,256]{3,2,1,0:T(8,128)(2,1)} %coarse_hbm.3, bf16[3,64,16,512]{3,2,1,0:T(8,128)(2,1)} %skip_hbm.3, bf16[2,2,64,128]{3,2,1,0:T(8,128)(2,1)} %up_w_hbm.3, bf16[3,3,64,128]{3,2,1,0:T(8,128)(2,1)} %w1_hbm.1, ...), custom_call_target="tpu_custom_call" | custom-call | tf_op jit(solution)/shard_map/inner_rows/pallas_call | solution.py:604
  29.4 0.0 collective-permute-done.3.across_ref
  29.4 0.0 copy-start.4
  29.4 0.0 collective-permute-done.2.far_ref
  29.4 0.0 copy-start.3
  29.4 8.7 %collective-permute-done.one_ref = bf16[3,3,64,512]{3,2,1,0:T(8,128)(2,1)S(1)} collective-permute-done((bf16[3,3,64,512]{3,2,1,0:T(8,128)(2,1)}, bf16[3,3,64,512]{3,2,1,0:T(8,128)(2,1)S(1)}, u32[]{:S(2)}, u32[]{:S(2)}) %collective-permute-start) | collective-permute-done | bytes 589856 | tf_op jit(solution)/shard_map/ppermute | solution.py:594
  38.2 0.0 copy-start.1
  38.2 0.0 collective-permute-done.1.two_ref
  38.2 0.0 all-to-all-done.recv_ref
  38.2 0.0 copy-start
  38.2 0.0 copy-done.4
  38.2 0.0 copy-done.3
  38.2 0.8 copy-done.1
  39.0 0.2 copy-done.2
  39.2 0.3 copy-done
  39.4 12.2 %edges_and_second.1 = (f32[3,8,16,512]{3,2,1,0:T(8,128)}, bf16[128,32,128]{2,1,0:T(8,128)(2,1)}) custom-call(bf16[3,16,64,512]{3,2,1,0:T(8,128)(2,1)} %get-tuple-element.12.first_hbm, f32[3,4,64,512]{3,2,1,0:T(8,128)} %get-tuple-element.13.part_hbm, f32[192,128]{1,0:T(8,128)} %get-tuple-element.14.cols_hbm, bf16[3,3,64,512]{3,2,1,0:T(8,128)(2,1)} %copy-done.1, ...), custom_call_target="tpu_custom_call" | custom-call | tf_op jit(solution)/shard_map/edges_and_second/pallas_call | solution.py:626
  51.7 29.3 %all_to_all.10.recv_ref = bf16[128,32,128]{2,1,0:T(8,128)(2,1)S(1)} all-to-all(bf16[128,32,128]{2,1,0:T(8,128)(2,1)} %get-tuple-element.21), channel_id=1, replica_groups=mesh['face'=4,'tile'=32] {'face','tile'}, dimensions={0} | all-to-all | bytes 2097152 | tf_op jit(solution)/shard_map/all_to_all | solution.py:660
  81.0 1.5 %ocean_slots.1 = f32[44,24,128]{2,1,0:T(8,128)} custom-call(bf16[128,32,128]{2,1,0:T(8,128)(2,1)S(1)} %all_to_all.10.recv_ref), custom_call_target="tpu_custom_call" | custom-call | tf_op jit(solution)/shard_map/ocean_slots/pallas_call | solution.py:661
  (1 shorter events, 0.0 us)
Async XLA Ops:
  5.4 32.8 %all-to-all-start = ((bf16[32,96,128]{2,1,0:T(8,128)(2,1)}), bf16[32,96,128]{2,1,0:T(8,128)(2,1)S(1)}, u32[]{:S(2)}, u32[]{:S(2)}) async-start(bf16[32,96,128]{2,1,0:T(8,128)(2,1)} %get-tuple-element.17), calls=%async_computation | async-start | bytes 1572864 | tf_op jit(solution)/shard_map/all_to_all | solution.py:601
  14.7 23.5 %collective-permute-start = (bf16[3,3,64,512]{3,2,1,0:T(8,128)(2,1)}, bf16[3,3,64,512]{3,2,1,0:T(8,128)(2,1)S(1)}, u32[]{:S(2)}, u32[]{:S(2)}) collective-permute-start(bf16[3,3,64,512]{3,2,1,0:T(8,128)(2,1)} %get-tuple-element.15), channel_id=1, source_target_pairs={{0,1},{1,0},{2,3},{3,2},{4,5},{5,4},{6,7},{7,6},{8,9},{9,8},{10,11... | collective-permute-start | bytes 1769480 | tf_op jit(solution)/shard_map/ppermute | solution.py:594
  16.6 21.6 %collective-permute-start.1 = (bf16[3,3,64,512]{3,2,1,0:T(8,128)(2,1)}, bf16[3,3,64,512]{3,2,1,0:T(8,128)(2,1)S(1)}, u32[]{:S(2)}, u32[]{:S(2)}) collective-permute-start(bf16[3,3,64,512]{3,2,1,0:T(8,128)(2,1)} %get-tuple-element.16), channel_id=1, source_target_pairs={{1,2},{2,1},{3,4},{4,3},{5,6},{6,5},{7,8},{8,7},{9,10},{10,9},{11,... | collective-permute-start | bytes 1769480 | tf_op jit(solution)/shard_map/ppermute | solution.py:595
  17.3 12.1 %collective-permute-start.2 = (bf16[192,128]{1,0:T(8,128)(2,1)}, bf16[192,128]{1,0:T(8,128)(2,1)S(1)}, u32[]{:S(2)}, u32[]{:S(2)}) collective-permute-start(bf16[192,128]{1,0:T(8,128)(2,1)} %get-tuple-element.18), channel_id=1, source_target_pairs={{31,127},{63,95},{95,63},{127,31}} | collective-permute-start | bytes 147464 | tf_op jit(solution)/shard_map/ppermute | solution.py:596
  17.9 11.5 %collective-permute-start.3 = (bf16[96,128]{1,0:T(8,128)(2,1)}, bf16[96,128]{1,0:T(8,128)(2,1)S(1)}, u32[]{:S(2)}, u32[]{:S(2)}) collective-permute-start(bf16[96,128]{1,0:T(8,128)(2,1)} %get-tuple-element.19), channel_id=1, source_target_pairs={{31,95},{63,127},{95,31},{127,63}} | collective-permute-start | bytes 73736 | tf_op jit(solution)/shard_map/ppermute | solution.py:597
  29.4 8.8 %copy-start.4 = (bf16[96,128]{1,0:T(8,128)(2,1)}, bf16[96,128]{1,0:T(8,128)(2,1)S(1)}, u32[]{:S(2)}) copy-start(bf16[96,128]{1,0:T(8,128)(2,1)S(1)} %collective-permute-done.3.across_ref) | copy-start | bytes 73732
  29.4 8.8 %copy-start.3 = (bf16[192,128]{1,0:T(8,128)(2,1)}, bf16[192,128]{1,0:T(8,128)(2,1)S(1)}, u32[]{:S(2)}) copy-start(bf16[192,128]{1,0:T(8,128)(2,1)S(1)} %collective-permute-done.2.far_ref) | copy-start | bytes 147460
  38.2 0.8 %copy-start.1 = (bf16[3,3,64,512]{3,2,1,0:T(8,128)(2,1)}, bf16[3,3,64,512]{3,2,1,0:T(8,128)(2,1)S(1)}, u32[]{:S(2)}) copy-start(bf16[3,3,64,512]{3,2,1,0:T(8,128)(2,1)S(1)} %collective-permute-done.one_ref) | copy-start | bytes 1769476
  38.2 1.0 %copy-start.2 = (bf16[3,3,64,512]{3,2,1,0:T(8,128)(2,1)}, bf16[3,3,64,512]{3,2,1,0:T(8,128)(2,1)S(1)}, u32[]{:S(2)}) copy-start(bf16[3,3,64,512]{3,2,1,0:T(8,128)(2,1)S(1)} %collective-permute-done.1.two_ref) | copy-start | bytes 1769476
  38.2 1.2 %copy-start = (bf16[32,96,128]{2,1,0:T(8,128)(2,1)}, bf16[32,96,128]{2,1,0:T(8,128)(2,1)S(1)}, u32[]{:S(2)}) copy-start(bf16[32,96,128]{2,1,0:T(8,128)(2,1)S(1)} %all-to-all-done.recv_ref) | copy-start | bytes 2359300

commit v3 on v2

--- a/solution.py
+++ b/solution.py
@@ -83,8 +83,8 @@
 
 
 def pack_kernel(
-    coarse_hbm, skip_hbm, one_hbm, two_hbm, send_hbm, col_ref, edge_ref,
-    coarse_ref, skip_ref, one_ref, two_ref, send_ref, skip_t, coarse_t, sems,
+    coarse_hbm, skip_hbm, up_w_hbm, w_hbm, up_bias_hbm, one_hbm, two_hbm, send_hbm, col_ref, edge_ref,
+    coarse_ref, skip_ref, up_w_ref, w_ref, up_bias_ref, one_ref, two_ref, send_ref, skip_t, coarse_t, sems,
 ):
     tile = lax.axis_index("tile")
     bottom = tile == lax.axis_size("tile") - 1
@@ -99,13 +99,24 @@
     def store_one(member):
         return [pltpu.make_async_copy(one_ref.at[member], one_hbm.at[member], sems.at[2, member])]
 
+    small = [
+        pltpu.make_async_copy(up_w_hbm, up_w_ref, sems.at[5, 0]),
+        pltpu.make_async_copy(w_hbm, w_ref, sems.at[5, 1]),
+        pltpu.make_async_copy(up_bias_hbm, up_bias_ref, sems.at[5, 2]),
+    ]
+    begin(small)
     for member in range(3):
         begin(loads(member))
+    finish(small)
+    up_w = up_rows(up_w_ref)
+    up_bias = wide(bias_column(up_bias_ref, 64), 4)
+    by_row = [row_taps(w_ref, r) for r in range(3)]
 
     def one(member, carry):
         finish(loads(member))
         pack_member(
-            member, bottom, even, coarse_ref, skip_ref, one_ref, two_ref, send_ref, col_ref, edge_ref, skip_t, coarse_t
+            member, bottom, even, up_w, up_bias, by_row,
+            coarse_ref, skip_ref, one_ref, two_ref, send_ref, col_ref, edge_ref, skip_t, coarse_t,
         )
 
         begin(store_one(member))
@@ -115,7 +126,7 @@
 
     @pl.when(bottom)
     def _():
-        two_ref[:, 0, :, :128] = edge_ref[...].reshape(3, 64, 128)
+        two_ref[:, :, :128] = edge_ref[...].reshape(3, 64, 128)
 
     store_two = pltpu.make_async_copy(two_ref, two_hbm, sems.at[3, 0])
     store_two.start()
@@ -138,20 +149,37 @@
 
 
 def pack_member(
-    member, bottom, even, coarse_ref, skip_ref, one_ref, two_ref, send_ref, col_ref, edge_ref, skip_t, coarse_t
+    member, bottom, even, up_w, up_bias, by_row,
+    coarse_ref, skip_ref, one_ref, two_ref, send_ref, col_ref, edge_ref, skip_t, coarse_t,
 ):
     own = pl.ds(pl.multiple_of(member * 32, 32), 32)
     rows = jnp.swapaxes(skip_ref[member], 0, 1)
     coarse_rows = jnp.swapaxes(coarse_ref[member], 0, 1)
 
-    def pair(row):
-        return jnp.concatenate([row[:64], row[64:]], axis=1)
-
-    top = (rows[0], rows[1], pair(coarse_rows[0]))
-    low = (rows[14], rows[15], pair(coarse_rows[7]))
-    for k in range(3):
-        one_ref[member, k] = jnp.where(even, low[k], top[k])
-        two_ref[member, k] = jnp.where(even, top[k], low[k])
+    def joined(coarse_row, pair):
+        fine = dot(up_w, spread(coarse_row.astype(F32)))
+        parts = [(fine[64 * a : 64 * a + 64] + up_bias).astype(BF) for a in range(2)]
+        return [jnp.concatenate([part, row], axis=0) for part, row in zip(parts, pair)]
+
+    lane64 = lanes_of((64, 128))
+
+    def outgoing(reached, own, pair):
+        ends = jnp.zeros((64, 128), F32)
+        for a, row in enumerate(pair):
+            end = row[:, 384:].astype(F32)
+            for h in range(2):
+                moved = pltpu.roll(end[64 * h : 64 * h + 64], 2 * a + h + 1, 1)
+                ends = jnp.where(lane64 == 2 * a + h, moved, ends)
+        return jnp.concatenate([reached, own, ends], axis=1).astype(BF)
+
+    pair = joined(coarse_rows[0], rows[0:2])
+    terms = dot(jnp.concatenate([by_row[2], by_row[1]], axis=0), taps(pair[0]))
+    top = outgoing(terms[:64], terms[64:] + dot(by_row[2], taps(pair[1])), pair)
+    pair = joined(coarse_rows[7], rows[14:16])
+    terms = dot(jnp.concatenate([by_row[0], by_row[1]], axis=0), taps(pair[1]))
+    low = outgoing(terms[:64], terms[64:] + dot(by_row[0], taps(pair[0])), pair)
+    one_ref[member] = jnp.where(even, low, top)
+    two_ref[member] = jnp.where(even, top, low)
 
     lane = lanes_of((128, 128))
     skip_cols = jnp.zeros((128, 128), F32)
@@ -289,11 +317,12 @@
 
 
 def edge_kernel(
-    first_hbm, part_hbm, cols_hbm, one_ref, two_ref, recv_ref, far_ref, across_ref,
+    first_hbm, part_hbm, cols_hbm, one_hbm, two_hbm, recv_hbm, far_hbm, across_hbm,
     up_w_hbm, w1_hbm, w2_hbm, head_hbm, up_bias_hbm, first_bias_hbm, second_bias_hbm, head_bias_hbm, mask_hbm,
-    target_hbm, flux_ref, send_ref,
+    target_hbm, flux_hbm, send_hbm,
     first_ref, part_ref, cols_ref, up_w_ref, w1_ref, w2_ref, head_ref, up_bias_ref, first_bias_ref,
-    second_bias_ref, head_bias_ref, mask_ref, target_ref, halo_skip, halo_coarse, piece_ref, rows_ref, second_ref, sems,
+    second_bias_ref, head_bias_ref, mask_ref, target_ref, terms_ref, ends_ref, piece_ref, second_ref,
+    one_ref, two_ref, recv_ref, far_ref, across_ref, flux_ref, send_ref, sems,
 ):
     tile = lax.axis_index("tile")
     bottom = tile == lax.axis_size("tile") - 1
@@ -322,40 +351,35 @@
                 (mask_hbm, mask_ref),
                 (target_hbm, target_ref),
                 (cols_hbm, cols_ref),
+                (one_hbm, one_ref),
+                (two_hbm, two_ref),
+                (across_hbm, across_ref),
+                (far_hbm, far_ref),
+                (recv_hbm.at[31], recv_ref.at[31]),
             ]
         )
     ]
-    begin(small)
-    for member in range(3):
-        begin(loads(member))
-
-    @pl.when(jnp.logical_not(bottom))
-    def _():
-        for member in range(3):
-            for a in range(2):
-                halo_skip[member, a] = jnp.where(even_tile, one_ref[member, a], two_ref[member, a])
-            both = jnp.where(even_tile, one_ref[member, 2], two_ref[member, 2]).astype(F32)
-            halo_coarse[member] = jnp.concatenate([both[:, :256], both[:, 256:]], axis=0)
-        piece_ref[...] = recv_ref[31].astype(F32)
+    chunks = pltpu.make_async_copy(
+        recv_hbm.at[pl.ds(0, 31)], recv_ref.at[pl.ds(0, 31)], sems.at[3, 0]
+    )
+
+    def store_flux(member):
+        return [pltpu.make_async_copy(flux_ref.at[member], flux_hbm.at[member], sems.at[3, 1 + member])]
 
     @pl.when(bottom)
     def _():
-        near, far = two_ref[:, 0, :, :128].reshape(192, 128), far_ref[...]
-        from_previous = jnp.where(even_face, far[:96], near[:96])
-        for member in range(3):
-            own = slice(32 * member, 32 * member + 32)
-            pieces = [recv_ref[j].astype(F32)[own] for j in range(31)]
-            pieces.append(from_previous.astype(F32)[own])
-            for q in range(4):
-                stacked = jnp.concatenate([pieces[8 * q + j][:16] for j in range(8)], axis=0).T.astype(BF)
-                halo_skip[member, 0, :, 128 * q : 128 * q + 128] = stacked[:64]
-                halo_skip[member, 1, :, 128 * q : 128 * q + 128] = stacked[64:]
-            for q in range(2):
-                stacked = jnp.concatenate([pieces[16 * q + j][16:24] for j in range(16)], axis=0).T
-                halo_coarse[member, :, 128 * q : 128 * q + 128] = stacked
-        piece_ref[...] = jnp.where(even_face, near[96:], far[96:]).astype(F32)
-
+        chunks.start()
+
+    begin(small)
+    begin(loads(0))
     finish(small)
+    begin(loads(1))
+    begin(loads(2))
+
+    @pl.when(bottom)
+    def _():
+        chunks.wait()
+
     up_bias = bias_column(up_bias_ref, 64)
     up_bias_wide = wide(up_bias, 4)
     first_bias = bias_column(first_bias_ref, 64)
@@ -369,27 +393,70 @@
     zero = jnp.zeros((128, 128), F32)
     ghost_rows = jnp.zeros((32, 128), F32)
 
-    up_w = up_rows(up_w_ref)
-    turned_up = jnp.concatenate(
-        [jnp.concatenate([up_w_ref[0, 1 - q], up_w_ref[1, 1 - q]], axis=1) for q in range(2)], axis=0
-    )
-    below_w = jnp.where(bottom, turned_up, up_w)
+    by_row = [row_taps(w1_ref, r) for r in range(3)]
+    above = jnp.where(even_tile, two_ref[...], one_ref[...])
+
+    @pl.when(jnp.logical_not(bottom))
+    def _():
+        below = jnp.where(even_tile, one_ref[...], two_ref[...]).astype(F32)
+        for member in range(3):
+            terms_ref[member, 2] = below[member, :, :512]
+            terms_ref[member, 3] = below[member, :, 512:1024]
+            ends_ref[member] = below[member, :, 1024:]
+        piece_ref[...] = recv_ref[31].astype(F32)
+
+    @pl.when(bottom)
+    def _():
+        near, far = two_ref[:, :, :128].reshape(192, 128), far_ref[...]
+        from_previous = jnp.where(even_face, far[:96], near[:96])
+        turned_up = jnp.concatenate(
+            [jnp.concatenate([up_w_ref[0, 1 - q], up_w_ref[1, 1 - q]], axis=1) for q in range(2)], axis=0
+        )
+        near_weight = jnp.concatenate([by_row[2], turned_taps(w1_ref, 1)], axis=0)
+        far_weight = turned_taps(w1_ref, 2)
+        for member in range(3):
+            own = slice(32 * member, 32 * member + 32)
+            pieces = [recv_ref[j].astype(F32)[own] for j in range(31)]
+            pieces.append(from_previous.astype(F32)[own])
+            skip = jnp.concatenate(
+                [
+                    jnp.concatenate([pieces[8 * q + j][:16] for j in range(8)], axis=0).T.astype(BF)
+                    for q in range(4)
+                ],
+                axis=1,
+            )
+            coarse = jnp.concatenate(
+                [
+                    jnp.concatenate([pieces[16 * q + j][16:24] for j in range(16)], axis=0).T
+                    for q in range(2)
+                ],
+                axis=1,
+            )
+            fine = dot(turned_up, spread(coarse))
+            beyond = [
+                jnp.concatenate(
+                    [(fine[64 * a : 64 * a + 64] + up_bias_wide).astype(BF), skip[64 * a : 64 * a + 64]], axis=0
+                )
+                for a in range(2)
+            ]
+            terms = dot(near_weight, taps(beyond[0]))
+            terms_ref[member, 2] = terms[:64]
+            terms_ref[member, 3] = terms[64:] + dot(far_weight, taps(beyond[1]))
+            ends_ref[member] = jnp.zeros((64, 128), F32)
+        piece_ref[...] = jnp.where(even_face, near[96:], far[96:]).astype(F32)
+
     edge = cols_ref[:128]
     for member in range(3):
-        both = jnp.where(even_tile, two_ref[member, 2], one_ref[member, 2]).astype(F32)
-        fine = dot(up_w, spread(jnp.concatenate([both[:, :256], both[:, 256:]], axis=0)))
-        fine_below = dot(below_w, spread(halo_coarse[member]))
-        for a in range(2):
-            upsampled = (fine[64 * a : 64 * a + 64] + up_bias_wide).astype(BF)
-            skip = jnp.where(even_tile, two_ref[member, a], one_ref[member, a])
-            row = jnp.concatenate([upsampled, skip], axis=0)
-            row = jnp.where(top, jnp.zeros_like(row), row)
-            upsampled = (fine_below[64 * a : 64 * a + 64] + up_bias_wide).astype(BF)
-            row_below = jnp.concatenate([upsampled, halo_skip[member, a]], axis=0)
-            for x, value in ((a, row), (18 + a, row_below)):
-                rows_ref[member, a if x < 2 else 2 + a] = value
-                end = pltpu.roll(value[:, 384:512].astype(F32), (32 * member + x + 1) % 128, 1)
-                edge = jnp.where(lane == 32 * member + x, end, edge)
+        end = above[member, :, 1024:].astype(F32)
+        terms_ref[member, 0] = above[member, :, 512:1024].astype(F32)
+        terms_ref[member, 1] = above[member, :, :512].astype(F32)
+        for x, ends in ((0, end), (18, ends_ref[member])):
+            for a in range(2):
+                target = 32 * member + x + a
+                moved = jnp.concatenate(
+                    [pltpu.roll(ends, (target - 2 * a - h) % 128, 1) for h in range(2)], axis=0
+                )
+                edge = jnp.where(lane == target, moved, edge)
 
     pixel = tile * ROWS - 2 + place
     piece = jnp.concatenate([piece_ref[...], ghost_rows], axis=0).T
@@ -444,8 +511,6 @@
     first_ghost = jnp.where(inside64, silu(summed + first_bias), jnp.zeros((64, 128), F32))
     last = silu(cols_ref[128:] + added)
 
-    by_row = [row_taps(w1_ref, r) for r in range(3)]
-    turned = [jnp.where(bottom, turned_taps(w1_ref, r), by_row[r]) for r in range(3)]
     second_weight = jnp.concatenate([row_taps(w2_ref, r) for r in range(3)], axis=0)
     head = head_ref[...]
     lane512 = lanes_of((64, COLS))
@@ -459,14 +524,9 @@
             return silu(summed + first_bias_wide).astype(BF)
 
         finish(loads(member))
-        term = dot(by_row[0], taps(rows_ref[member, 0]))
-        terms = dot(jnp.concatenate([by_row[1], by_row[0]], axis=0), taps(rows_ref[member, 1]))
-        row_m1 = finished(part_ref[member, 0] + term + terms[:64], -1)
-        row_0 = finished(part_ref[member, 1] + terms[64:], 0)
-        term = dot(turned[2], taps(rows_ref[member, 3]))
-        terms = dot(jnp.concatenate([turned[1], by_row[2]], axis=0), taps(rows_ref[member, 2]))
-        row_15 = finished(part_ref[member, 2] + terms[64:], 15)
-        row_16 = finished(part_ref[member, 3] + term + terms[:64], 16)
+        row_m1, row_0, row_15, row_16 = (
+            finished(part_ref[member, k] + terms_ref[member, k], x) for k, x in enumerate((-1, 0, 15, 16))
+        )
         outer = {-1: jnp.where(top, jnp.zeros_like(row_m1), row_m1), 0: row_0, 15: row_15, 16: row_16}
 
         before = [None, None]
@@ -492,6 +552,7 @@
                 second_ref[n] = silu(done + second_bias_wide).astype(BF)
         for n in range(ROWS):
             flux_ref[member, :, n, :] = dot(head, second_ref[n]) + head_bias
+        begin(store_flux(member))
         return carry
 
     lax.fori_loop(0, 3, one, 0)
@@ -517,6 +578,11 @@
     slots = jnp.broadcast_to(slots, (128, 128)).astype(BF)
     packed += [slots] * 8
     send_ref[...] = jnp.swapaxes(jnp.stack(packed, axis=0), 0, 1)
+    send = pltpu.make_async_copy(send_ref, send_hbm, sems.at[3, 4])
+    send.start()
+    for member in range(3):
+        finish(store_flux(member))
+    send.wait()
 
 
 def unpack_kernel(recv_ref, out_ref):
@@ -556,13 +622,14 @@
     params = pltpu.CompilerParams(vmem_limit_bytes=VMEM_LIMIT)
     sds = jax.ShapeDtypeStruct
 
+    up_bias, first_bias, second_bias = (b.reshape(1, 64) for b in (up_bias, first_bias, second_bias))
     one, two, send, col, edges = pl.pallas_call(
         pack_kernel,
-        in_specs=hbm(2),
+        in_specs=hbm(5),
         out_specs=hbm(3) + vmem(2),
         out_shape=[
-            sds((3, 3, 64, 512), BF),
-            sds((3, 3, 64, 512), BF),
+            sds((3, 64, 1152), BF),
+            sds((3, 64, 1152), BF),
             sds((32, 96, 128), BF),
             sds((96, 128), BF),
             sds((192, 128), BF),
@@ -570,16 +637,19 @@
         scratch_shapes=[
             pltpu.VMEM((3, 128, 8, 256), BF),
             pltpu.VMEM((3, 64, 16, 512), BF),
-            pltpu.VMEM((3, 3, 64, 512), BF),
-            pltpu.VMEM((3, 3, 64, 512), BF),
+            pltpu.VMEM((2, 2, 64, 128), BF),
+            pltpu.VMEM((3, 3, 64, 128), BF),
+            pltpu.VMEM((1, 64), F32),
+            pltpu.VMEM((3, 64, 1152), BF),
+            pltpu.VMEM((3, 64, 1152), BF),
             pltpu.VMEM((32, 96, 128), BF),
             pltpu.VMEM((544, 128), F32),
             pltpu.VMEM((272, 128), F32),
-            pltpu.SemaphoreType.DMA((5, 3)),
+            pltpu.SemaphoreType.DMA((6, 3)),
         ],
         compiler_params=params,
         name="pack_edges",
-    )(coarse_features, skip_features)
+    )(coarse_features, skip_features, up_weight, first_weight, up_bias)
 
     last = tiles - 1
 
@@ -600,7 +670,6 @@
     ]
     recv = lax.all_to_all(send, both, 0, 0, axis_index_groups=groups, tiled=True)
 
-    up_bias, first_bias, second_bias = (b.reshape(1, 64) for b in (up_bias, first_bias, second_bias))
     first, parts, cols = pl.pallas_call(
         inner_kernel,
         in_specs=hbm(6),
@@ -625,8 +694,8 @@
 
     flux, send = pl.pallas_call(
         edge_kernel,
-        in_specs=hbm(3) + vmem(5) + hbm(10),
-        out_specs=vmem(2),
+        in_specs=hbm(18),
+        out_specs=hbm(2),
         out_shape=[sds((3, 8, 16, 512), F32), sds((devices, 32, 128), BF)],
         scratch_shapes=[
             pltpu.VMEM((3, 16, 64, 512), BF),
@@ -642,12 +711,18 @@
             pltpu.VMEM((1, 8), F32),
             pltpu.VMEM((16, 512), jnp.int32),
             pltpu.VMEM((1, 64), jnp.int32),
-            pltpu.VMEM((3, 2, 64, 512), BF),
-            pltpu.VMEM((3, 128, 256), F32),
+            pltpu.VMEM((3, 4, 64, 512), F32),
+            pltpu.VMEM((3, 64, 128), F32),
             pltpu.VMEM((96, 128), F32),
-            pltpu.VMEM((3, 4, 128, 512), BF),
             pltpu.VMEM((16, 64, 512), BF),
-            pltpu.SemaphoreType.DMA((3, 11)),
+            pltpu.VMEM((3, 64, 1152), BF),
+            pltpu.VMEM((3, 64, 1152), BF),
+            pltpu.VMEM((32, 96, 128), BF),
+            pltpu.VMEM((192, 128), BF),
+            pltpu.VMEM((96, 128), BF),
+            pltpu.VMEM((3, 8, 16, 512), F32),
+            pltpu.VMEM((128, 32, 128), BF),
+            pltpu.SemaphoreType.DMA((4, 16)),
         ],
         compiler_params=params,
         name="edges_and_second",

time: 82.9 us -> 81.3 us (0.981)
  waiting for transfers between devices: 8.76 us -> 5.53 us
  blocking collectives: 29.3 us -> 31.7 us
    ppermute x1, waiting for transfers between devices: 8.75 us -> 5.52 us  [shards(): got_one = lax.ppermute(one, both, first_pairs)]
    all_to_all x1, blocking collectives: 29.3 us -> 31.7 us  [shards(): got = lax.all_to_all(send, both, 0, 0, tiled=True)]
where the time goes in v3:
time: 81.3 us; the launch traced here: 80.9 us
  blocking collectives  31.7 us (39%)
  Pallas kernels  28.6 us (35%)
  starting transfers between devices  13.1 us (16%)
  waiting for transfers between devices  5.53 us (7%)
  local copies, waits for them, and re-layouts  1.15 us (1%)
    all_to_all x1, blocking collectives, shards(): got = lax.all_to_all(send, both, 0, 0, tiled=True)  31.7 us
    pallas_call x1, Pallas kernels, shards(): pl.pallas_call(inner_kernel, in_specs=hbm(6), out_specs=hbm(3), out_shape...  10.8 us
    pallas_call x1, Pallas kernels, shards(): pl.pallas_call(edge_kernel, in_specs=hbm(18), out_specs=hbm(2), out_shape...  9.56 us
    all_to_all x1, starting transfers between devices, shards(): lax.all_to_all(send, both, 0, 0, axis_index_groups=groups, tiled=True)  9.27 us
    pallas_call x1, Pallas kernels, shards(): pl.pallas_call(pack_kernel, in_specs=hbm(5), out_specs=hbm(3) + vmem(2),...  6.75 us
    ppermute x1, waiting for transfers between devices, shards(): got_one = lax.ppermute(one, both, first_pairs)  5.52 us
    ppermute x1, starting transfers between devices, shards(): got_one = lax.ppermute(one, both, first_pairs)  1.87 us
  transfers between devices with their start and end apart: 5, of which 1 were waited for; matrix products, arithmetic and copies ran while one was open for 0% of the time, Pallas kernels for 13%

profile of v3, /device:TPU:0, one launch (start us, length us, event | category | flops | bytes accessed | tf_op | source)
XLA Modules:
  0.0 80.9 jit_solution(931834771311224637)
XLA Ops:
  0.6 6.7 %pack_edges.1 = (bf16[3,64,1152]{2,1,0:T(8,128)(2,1)}, bf16[3,64,1152]{2,1,0:T(8,128)(2,1)}, bf16[32,96,128]{2,1,0:T(8,128)(2,1)}, bf16[96,128]{1,0:T(8,128)(2,1)}, bf16[192,128]{1,0:T(8,128)(2,1)}) custom-call(bf16[3,128,8,256]{3,2,1,0:T(8,128)(2,1)} %coarse_hbm.3, bf16[3,64,16,512]{3,2,1,0:T(8,128)(2,1)} %skip_hbm.3, bf16[2,2,64,128]{3,2,1,0:T(8,128)(2,1)} %up_w_hbm.5, ...), custom_call_target="tpu_custom_call" | custom-call | tf_op jit(solution)/shard_map/pack_edges/pallas_call | solution.py:626
  7.4 9.3 %all-to-all-start = ((bf16[32,96,128]{2,1,0:T(8,128)(2,1)}), bf16[32,96,128]{2,1,0:T(8,128)(2,1)S(1)}, u32[]{:S(2)}, u32[]{:S(2)}) async-start(bf16[32,96,128]{2,1,0:T(8,128)(2,1)} %get-tuple-element.17), calls=%async_computation | async-start | bytes 1572864 | tf_op jit(solution)/shard_map/all_to_all | solution.py:671
  16.7 1.9 %collective-permute-start = (bf16[3,64,1152]{2,1,0:T(8,128)(2,1)}, bf16[3,64,1152]{2,1,0:T(8,128)(2,1)S(1)}, u32[]{:S(2)}, u32[]{:S(2)}) collective-permute-start(bf16[3,64,1152]{2,1,0:T(8,128)(2,1)} %get-tuple-element.15), channel_id=1, source_target_pairs={{0,1},{1,0},{2,3},{3,2},{4,5},{5,4},{6,7},{7,6},{8,9},{9,8},{10,11... | collective-permute-start | bytes 1327112 | tf_op jit(solution)/shard_map/ppermute | solution.py:664
  18.5 0.7 collective-permute-start.1
  19.2 0.7 collective-permute-start.2
  19.9 0.7 collective-permute-start.3
  20.6 10.8 %inner_rows.1 = (bf16[3,16,64,512]{3,2,1,0:T(8,128)(2,1)}, f32[3,4,64,512]{3,2,1,0:T(8,128)}, f32[192,128]{1,0:T(8,128)}) custom-call(bf16[3,128,8,256]{3,2,1,0:T(8,128)(2,1)} %coarse_hbm.3, bf16[3,64,16,512]{3,2,1,0:T(8,128)(2,1)} %skip_hbm.3, bf16[2,2,64,128]{3,2,1,0:T(8,128)(2,1)} %up_w_hbm.5, bf16[3,3,64,128]{3,2,1,0:T(8,128)(2,1)} %w1_hbm.1, ...), custom_call_target="tpu_custom_call" | custom-call | tf_op jit(solution)/shard_map/inner_rows/pallas_call | solution.py:673
  31.4 0.0 collective-permute-done.3.across_hbm
  31.4 0.0 copy-start.4
  31.4 0.0 collective-permute-done.2.far_hbm
  31.4 0.0 copy-start.3
  31.4 5.5 %collective-permute-done.one_hbm = bf16[3,64,1152]{2,1,0:T(8,128)(2,1)S(1)} collective-permute-done((bf16[3,64,1152]{2,1,0:T(8,128)(2,1)}, bf16[3,64,1152]{2,1,0:T(8,128)(2,1)S(1)}, u32[]{:S(2)}, u32[]{:S(2)}) %collective-permute-start) | collective-permute-done | bytes 442400 | tf_op jit(solution)/shard_map/ppermute | solution.py:664
  36.9 0.0 copy-start.1
  36.9 0.0 collective-permute-done.1.two_hbm
  36.9 0.0 all-to-all-done.recv_hbm
  36.9 0.0 copy-start
  36.9 0.0 copy-done.4
  37.0 0.0 copy-done.3
  37.0 0.7 copy-done.1
  37.7 0.2 copy-done.2
  37.8 0.3 copy-done
  38.1 9.6 %edges_and_second.1 = (f32[3,8,16,512]{3,2,1,0:T(8,128)}, bf16[128,32,128]{2,1,0:T(8,128)(2,1)}) custom-call(bf16[3,16,64,512]{3,2,1,0:T(8,128)(2,1)} %get-tuple-element.12.first_hbm, f32[3,4,64,512]{3,2,1,0:T(8,128)} %get-tuple-element.13.part_hbm, f32[192,128]{1,0:T(8,128)} %get-tuple-element.14.cols_hbm, bf16[3,64,1152]{2,1,0:T(8,128)(2,1)} %copy-done.1, ...), custom_call_target="tpu_custom_call" | custom-call | tf_op jit(solution)/shard_map/edges_and_second/pallas_call | solution.py:695
  47.7 31.7 %all_to_all.10.recv_ref = bf16[128,32,128]{2,1,0:T(8,128)(2,1)S(1)} all-to-all(bf16[128,32,128]{2,1,0:T(8,128)(2,1)} %get-tuple-element.21), channel_id=1, replica_groups=mesh['face'=4,'tile'=32] {'face','tile'}, dimensions={0} | all-to-all | bytes 2097152 | tf_op jit(solution)/shard_map/all_to_all | solution.py:735
  79.4 1.5 %ocean_slots.1 = f32[44,24,128]{2,1,0:T(8,128)} custom-call(bf16[128,32,128]{2,1,0:T(8,128)(2,1)S(1)} %all_to_all.10.recv_ref), custom_call_target="tpu_custom_call" | custom-call | tf_op jit(solution)/shard_map/ocean_slots/pallas_call | solution.py:736
  (1 shorter events, 0.0 us)
Async XLA Ops:
  7.4 29.5 %all-to-all-start = ((bf16[32,96,128]{2,1,0:T(8,128)(2,1)}), bf16[32,96,128]{2,1,0:T(8,128)(2,1)S(1)}, u32[]{:S(2)}, u32[]{:S(2)}) async-start(bf16[32,96,128]{2,1,0:T(8,128)(2,1)} %get-tuple-element.17), calls=%async_computation | async-start | bytes 1572864 | tf_op jit(solution)/shard_map/all_to_all | solution.py:671
  16.7 20.3 %collective-permute-start = (bf16[3,64,1152]{2,1,0:T(8,128)(2,1)}, bf16[3,64,1152]{2,1,0:T(8,128)(2,1)S(1)}, u32[]{:S(2)}, u32[]{:S(2)}) collective-permute-start(bf16[3,64,1152]{2,1,0:T(8,128)(2,1)} %get-tuple-element.15), channel_id=1, source_target_pairs={{0,1},{1,0},{2,3},{3,2},{4,5},{5,4},{6,7},{7,6},{8,9},{9,8},{10,11... | collective-permute-start | bytes 1327112 | tf_op jit(solution)/shard_map/ppermute | solution.py:664
  18.5 18.4 %collective-permute-start.1 = (bf16[3,64,1152]{2,1,0:T(8,128)(2,1)}, bf16[3,64,1152]{2,1,0:T(8,128)(2,1)S(1)}, u32[]{:S(2)}, u32[]{:S(2)}) collective-permute-start(bf16[3,64,1152]{2,1,0:T(8,128)(2,1)} %get-tuple-element.16), channel_id=1, source_target_pairs={{1,2},{2,1},{3,4},{4,3},{5,6},{6,5},{7,8},{8,7},{9,10},{10,9},{11,... | collective-permute-start | bytes 1327112 | tf_op jit(solution)/shard_map/ppermute | solution.py:665
  19.2 12.2 %collective-permute-start.2 = (bf16[192,128]{1,0:T(8,128)(2,1)}, bf16[192,128]{1,0:T(8,128)(2,1)S(1)}, u32[]{:S(2)}, u32[]{:S(2)}) collective-permute-start(bf16[192,128]{1,0:T(8,128)(2,1)} %get-tuple-element.18), channel_id=1, source_target_pairs={{31,127},{63,95},{95,63},{127,31}} | collective-permute-start | bytes 147464 | tf_op jit(solution)/shard_map/ppermute | solution.py:666
  19.9 11.5 %collective-permute-start.3 = (bf16[96,128]{1,0:T(8,128)(2,1)}, bf16[96,128]{1,0:T(8,128)(2,1)S(1)}, u32[]{:S(2)}, u32[]{:S(2)}) collective-permute-start(bf16[96,128]{1,0:T(8,128)(2,1)} %get-tuple-element.19), channel_id=1, source_target_pairs={{31,95},{63,127},{95,31},{127,63}} | collective-permute-start | bytes 73736 | tf_op jit(solution)/shard_map/ppermute | solution.py:667
  31.4 5.6 %copy-start.4 = (bf16[96,128]{1,0:T(8,128)(2,1)}, bf16[96,128]{1,0:T(8,128)(2,1)S(1)}, u32[]{:S(2)}) copy-start(bf16[96,128]{1,0:T(8,128)(2,1)S(1)} %collective-permute-done.3.across_hbm) | copy-start | bytes 73732
  31.4 5.6 %copy-start.3 = (bf16[192,128]{1,0:T(8,128)(2,1)}, bf16[192,128]{1,0:T(8,128)(2,1)S(1)}, u32[]{:S(2)}) copy-start(bf16[192,128]{1,0:T(8,128)(2,1)S(1)} %collective-permute-done.2.far_hbm) | copy-start | bytes 147460
  36.9 0.8 copy-start.1
  36.9 0.9 %copy-start.2 = (bf16[3,64,1152]{2,1,0:T(8,128)(2,1)}, bf16[3,64,1152]{2,1,0:T(8,128)(2,1)S(1)}, u32[]{:S(2)}) copy-start(bf16[3,64,1152]{2,1,0:T(8,128)(2,1)S(1)} %collective-permute-done.1.two_hbm) | copy-start | bytes 1327108
  36.9 1.2 %copy-start = (bf16[32,96,128]{2,1,0:T(8,128)(2,1)}, bf16[32,96,128]{2,1,0:T(8,128)(2,1)S(1)}, u32[]{:S(2)}) copy-start(bf16[32,96,128]{2,1,0:T(8,128)(2,1)S(1)} %all-to-all-done.recv_hbm) | copy-start | bytes 2359300

commit v4 on v3

--- a/solution.py
+++ b/solution.py
@@ -96,8 +96,12 @@
             pltpu.make_async_copy(coarse_hbm.at[member], coarse_ref.at[member], sems.at[1, member]),
         ]
 
-    def store_one(member):
-        return [pltpu.make_async_copy(one_ref.at[member], one_hbm.at[member], sems.at[2, member])]
+    def stores(member):
+        part = pl.ds(8 * member, 8)
+        return [
+            pltpu.make_async_copy(one_ref.at[part], one_hbm.at[part], sems.at[2, member]),
+            pltpu.make_async_copy(two_ref.at[part], two_hbm.at[part], sems.at[3, member]),
+        ]
 
     small = [
         pltpu.make_async_copy(up_w_hbm, up_w_ref, sems.at[5, 0]),
@@ -114,22 +118,33 @@
 
     def one(member, carry):
         finish(loads(member))
-        pack_member(
+        one_ends, two_ends = pack_member(
             member, bottom, even, up_w, up_bias, by_row,
             coarse_ref, skip_ref, one_ref, two_ref, send_ref, col_ref, edge_ref, skip_t, coarse_t,
         )
 
-        begin(store_one(member))
-        return carry
-
-    lax.fori_loop(0, 3, one, 0)
+        @pl.when(member < 2)
+        def _():
+            begin(stores(member))
+
+        return carry[0] + one_ends, carry[1] + two_ends
+
+    nothing = jnp.zeros((64, 128), F32)
+    one_ends, two_ends = lax.fori_loop(0, 3, one, (nothing, nothing))
+    one_ref[24] = one_ends.astype(BF)
+    two_ref[24] = two_ends.astype(BF)
 
     @pl.when(bottom)
     def _():
-        two_ref[:, :, :128] = edge_ref[...].reshape(3, 64, 128)
-
-    store_two = pltpu.make_async_copy(two_ref, two_hbm, sems.at[3, 0])
-    store_two.start()
+        for k in range(3):
+            two_ref[16 + k] = edge_ref[64 * k : 64 * k + 64, :]
+
+    rest_of = pl.ds(16, 9)
+    tails = [
+        pltpu.make_async_copy(one_ref.at[rest_of], one_hbm.at[rest_of], sems.at[2, 2]),
+        pltpu.make_async_copy(two_ref.at[rest_of], two_hbm.at[rest_of], sems.at[3, 2]),
+    ]
+    begin(tails)
     ends = pltpu.make_async_copy(send_ref.at[31], send_hbm.at[31], sems.at[4, 0])
     rest = pltpu.make_async_copy(send_ref.at[pl.ds(0, 31)], send_hbm.at[pl.ds(0, 31)], sems.at[4, 1])
     ends.start()
@@ -138,9 +153,9 @@
     def _():
         rest.start()
 
-    for member in range(3):
-        finish(store_one(member))
-    store_two.wait()
+    for member in range(2):
+        finish(stores(member))
+    finish(tails)
     ends.wait()
 
     @pl.when(bottom)
@@ -170,7 +185,7 @@
             for h in range(2):
                 moved = pltpu.roll(end[64 * h : 64 * h + 64], 2 * a + h + 1, 1)
                 ends = jnp.where(lane64 == 2 * a + h, moved, ends)
-        return jnp.concatenate([reached, own, ends], axis=1).astype(BF)
+        return jnp.concatenate([reached, own], axis=1).astype(BF), pltpu.roll(ends, 4 * member, 1)
 
     pair = joined(coarse_rows[0], rows[0:2])
     terms = dot(jnp.concatenate([by_row[2], by_row[1]], axis=0), taps(pair[0]))
@@ -178,8 +193,12 @@
     pair = joined(coarse_rows[7], rows[14:16])
     terms = dot(jnp.concatenate([by_row[0], by_row[1]], axis=0), taps(pair[1]))
     low = outgoing(terms[:64], terms[64:] + dot(by_row[0], taps(pair[0])), pair)
-    one_ref[member] = jnp.where(even, low, top)
-    two_ref[member] = jnp.where(even, top, low)
+    for target, kept in ((one_ref, (low, top)), (two_ref, (top, low))):
+        terms = jnp.where(even, kept[0][0], kept[1][0])
+        for k in range(8):
+            target[8 * member + k] = terms[:, 128 * k : 128 * k + 128]
+    one_ends = jnp.where(even, low[1], top[1])
+    two_ends = jnp.where(even, top[1], low[1])
 
     lane = lanes_of((128, 128))
     skip_cols = jnp.zeros((128, 128), F32)
@@ -218,6 +237,8 @@
                 send_ref[j, own, :] = part
             else:
                 edge_ref[pl.ds(pl.multiple_of(96 + member * 32, 32), 32), :] = part
+
+    return one_ends, two_ends
 
 
 def inner_kernel(
@@ -395,19 +416,21 @@
 
     by_row = [row_taps(w1_ref, r) for r in range(3)]
     above = jnp.where(even_tile, two_ref[...], one_ref[...])
+    above = jnp.where(top, jnp.zeros_like(above), above)
 
     @pl.when(jnp.logical_not(bottom))
     def _():
         below = jnp.where(even_tile, one_ref[...], two_ref[...]).astype(F32)
         for member in range(3):
-            terms_ref[member, 2] = below[member, :, :512]
-            terms_ref[member, 3] = below[member, :, 512:1024]
-            ends_ref[member] = below[member, :, 1024:]
+            for k in range(4):
+                terms_ref[member, 2, :, 128 * k : 128 * k + 128] = below[8 * member + k]
+                terms_ref[member, 3, :, 128 * k : 128 * k + 128] = below[8 * member + 4 + k]
+            ends_ref[member] = pltpu.roll(below[24], (128 - 4 * member) % 128, 1)
         piece_ref[...] = recv_ref[31].astype(F32)
 
     @pl.when(bottom)
     def _():
-        near, far = two_ref[:, :, :128].reshape(192, 128), far_ref[...]
+        near, far = two_ref[16:19].reshape(192, 128), far_ref[...]
         from_previous = jnp.where(even_face, far[:96], near[:96])
         turned_up = jnp.concatenate(
             [jnp.concatenate([up_w_ref[0, 1 - q], up_w_ref[1, 1 - q]], axis=1) for q in range(2)], axis=0
@@ -447,9 +470,10 @@
 
     edge = cols_ref[:128]
     for member in range(3):
-        end = above[member, :, 1024:].astype(F32)
-        terms_ref[member, 0] = above[member, :, 512:1024].astype(F32)
-        terms_ref[member, 1] = above[member, :, :512].astype(F32)
+        end = pltpu.roll(above[24].astype(F32), (128 - 4 * member) % 128, 1)
+        for k in range(4):
+            terms_ref[member, 0, :, 128 * k : 128 * k + 128] = above[8 * member + 4 + k].astype(F32)
+            terms_ref[member, 1, :, 128 * k : 128 * k + 128] = above[8 * member + k].astype(F32)
         for x, ends in ((0, end), (18, ends_ref[member])):
             for a in range(2):
                 target = 32 * member + x + a
@@ -577,12 +601,17 @@
     slots = jnp.sum(by_pixel_row.astype(F32) * slots.astype(F32), axis=1, keepdims=True)
     slots = jnp.broadcast_to(slots, (128, 128)).astype(BF)
     packed += [slots] * 8
-    send_ref[...] = jnp.swapaxes(jnp.stack(packed, axis=0), 0, 1)
-    send = pltpu.make_async_copy(send_ref, send_hbm, sems.at[3, 4])
-    send.start()
+    packed = jnp.stack(packed, axis=0)
+    sends = []
+    for k in range(2):
+        part = slice(64 * k, 64 * k + 64)
+        send_ref[part] = jnp.swapaxes(packed[:, part], 0, 1)
+        half = pl.ds(64 * k, 64)
+        sends.append(pltpu.make_async_copy(send_ref.at[half], send_hbm.at[half], sems.at[3, 4 + k]))
+        sends[k].start()
     for member in range(3):
         finish(store_flux(member))
-    send.wait()
+    finish(sends)
 
 
 def unpack_kernel(recv_ref, out_ref):
@@ -628,8 +657,8 @@
         in_specs=hbm(5),
         out_specs=hbm(3) + vmem(2),
         out_shape=[
-            sds((3, 64, 1152), BF),
-            sds((3, 64, 1152), BF),
+            sds((25, 64, 128), BF),
+            sds((25, 64, 128), BF),
             sds((32, 96, 128), BF),
             sds((96, 128), BF),
             sds((192, 128), BF),
@@ -640,8 +669,8 @@
             pltpu.VMEM((2, 2, 64, 128), BF),
             pltpu.VMEM((3, 3, 64, 128), BF),
             pltpu.VMEM((1, 64), F32),
-            pltpu.VMEM((3, 64, 1152), BF),
-            pltpu.VMEM((3, 64, 1152), BF),
+            pltpu.VMEM((25, 64, 128), BF),
+            pltpu.VMEM((25, 64, 128), BF),
             pltpu.VMEM((32, 96, 128), BF),
             pltpu.VMEM((544, 128), F32),
             pltpu.VMEM((272, 128), F32),
@@ -662,9 +691,9 @@
     first_pairs = [(s + t, s + (t ^ 1)) for s in strips for t in range(tiles)]
     second_pairs = [(s + t, s + ((t - 1) ^ 1) + 1) for s in strips for t in range(1, last)]
     got_one = lax.ppermute(one, both, first_pairs)
-    got_two = lax.ppermute(two, both, second_pairs + swapped(1))
-    far = lax.ppermute(edges, both, swapped(3))
-    across = lax.ppermute(col, both, swapped(2))
+    got_two = lax.ppermute(two, both, second_pairs + swapped(1) + [(f * tiles, (f ^ 1) * tiles) for f in range(faces)])
+    far = lax.ppermute(edges, "face", [(f, f ^ 3) for f in range(faces)])
+    across = lax.ppermute(col, "face", [(f, f ^ 2) for f in range(faces)])
     groups = [
         [f * tiles + t for t in range(last)] + [((f + 1) % faces) * tiles + last] for f in range(faces)
     ]
@@ -715,8 +744,8 @@
             pltpu.VMEM((3, 64, 128), F32),
             pltpu.VMEM((96, 128), F32),
             pltpu.VMEM((16, 64, 512), BF),
-            pltpu.VMEM((3, 64, 1152), BF),
-            pltpu.VMEM((3, 64, 1152), BF),
+            pltpu.VMEM((25, 64, 128), BF),
+            pltpu.VMEM((25, 64, 128), BF),
             pltpu.VMEM((32, 96, 128), BF),
             pltpu.VMEM((192, 128), BF),
             pltpu.VMEM((96, 128), BF),

time: 81.3 us -> 80.6 us (level)
  waiting for transfers between devices: 5.53 us -> 2.26 us
  starting transfers between devices: 13.1 us -> 15.8 us
    ppermute x1, waiting for transfers between devices: 5.52 us -> 2.25 us  [shards(): got_one = lax.ppermute(one, both, first_pairs)]
    ppermute x3, starting transfers between devices: 2 us -> 4.61 us  [the longest x1 1.6 us: shards(): across = lax.ppermute(col, 'face', [(f, f ^ 2) for f in range(faces)])]
where the time goes in v4:
time: 80.6 us; the launch traced here: 80.2 us
  blocking collectives  31.7 us (39%)
  Pallas kernels  28.7 us (36%)
  starting transfers between devices  15.8 us (20%)
  waiting for transfers between devices  2.26 us (3%)
  local copies, waits for them, and re-layouts  1.13 us (1%)
    all_to_all x1, blocking collectives, shards(): got = lax.all_to_all(send, both, 0, 0, tiled=True)  31.7 us
    pallas_call x1, Pallas kernels, shards(): pl.pallas_call(inner_kernel, in_specs=hbm(6), out_specs=hbm(3), out_shape...  10.8 us
    pallas_call x1, Pallas kernels, shards(): pl.pallas_call(edge_kernel, in_specs=hbm(18), out_specs=hbm(2), out_shape...  9.56 us
    all_to_all x1, starting transfers between devices, shards(): lax.all_to_all(send, both, 0, 0, axis_index_groups=groups, tiled=True)  9.27 us
    pallas_call x1, Pallas kernels, shards(): pl.pallas_call(pack_kernel, in_specs=hbm(5), out_specs=hbm(3) + vmem(2),...  6.81 us
    ppermute x1, waiting for transfers between devices, shards(): got_one = lax.ppermute(one, both, first_pairs)  2.25 us
    ppermute x1, starting transfers between devices, shards(): got_one = lax.ppermute(one, both, first_pairs)  1.87 us
  transfers between devices with their start and end apart: 5, of which 1 were waited for; matrix products, arithmetic and copies ran while one was open for 0% of the time, Pallas kernels for 13%

profile of v4, /device:TPU:0, one launch (start us, length us, event | category | flops | bytes accessed | tf_op | source)
XLA Modules:
  0.0 80.2 jit_solution(6173355552831758456)
XLA Ops:
  0.6 6.8 %pack_edges.1 = (bf16[25,64,128]{2,1,0:T(8,128)(2,1)}, bf16[25,64,128]{2,1,0:T(8,128)(2,1)}, bf16[32,96,128]{2,1,0:T(8,128)(2,1)}, bf16[96,128]{1,0:T(8,128)(2,1)}, bf16[192,128]{1,0:T(8,128)(2,1)}) custom-call(bf16[3,128,8,256]{3,2,1,0:T(8,128)(2,1)} %coarse_hbm.3, bf16[3,64,16,512]{3,2,1,0:T(8,128)(2,1)} %skip_hbm.3, bf16[2,2,64,128]{3,2,1,0:T(8,128)(2,1)} %up_w_hbm.5, ...), custom_call_target="tpu_custom_call" | custom-call | tf_op jit(solution)/shard_map/pack_edges/pallas_call | solution.py:655
  7.4 9.3 %all-to-all-start = ((bf16[32,96,128]{2,1,0:T(8,128)(2,1)}), bf16[32,96,128]{2,1,0:T(8,128)(2,1)S(1)}, u32[]{:S(2)}, u32[]{:S(2)}) async-start(bf16[32,96,128]{2,1,0:T(8,128)(2,1)} %get-tuple-element.17), calls=%async_computation | async-start | bytes 1572864 | tf_op jit(solution)/shard_map/all_to_all | solution.py:700
  16.7 1.9 %collective-permute-start = (bf16[25,64,128]{2,1,0:T(8,128)(2,1)}, bf16[25,64,128]{2,1,0:T(8,128)(2,1)S(1)}, u32[]{:S(2)}, u32[]{:S(2)}) collective-permute-start(bf16[25,64,128]{2,1,0:T(8,128)(2,1)} %get-tuple-element.15), channel_id=1, source_target_pairs={{0,1},{1,0},{2,3},{3,2},{4,5},{5,4},{6,7},{7,6},{8,9},{9,8},{10,11... | collective-permute-start | bytes 1228808 | tf_op jit(solution)/shard_map/ppermute | solution.py:693
  18.6 1.5 %collective-permute-start.1 = (bf16[25,64,128]{2,1,0:T(8,128)(2,1)}, bf16[25,64,128]{2,1,0:T(8,128)(2,1)S(1)}, u32[]{:S(2)}, u32[]{:S(2)}) collective-permute-start(bf16[25,64,128]{2,1,0:T(8,128)(2,1)} %get-tuple-element.16), channel_id=1, source_target_pairs={{1,2},{2,1},{3,4},{4,3},{5,6},{6,5},{7,8},{8,7},{9,10},{10,9},{11,... | collective-permute-start | bytes 1228808 | tf_op jit(solution)/shard_map/ppermute | solution.py:694
  20.1 1.5 %collective-permute-start.2 = (bf16[192,128]{1,0:T(8,128)(2,1)}, bf16[192,128]{1,0:T(8,128)(2,1)S(1)}, u32[]{:S(2)}, u32[]{:S(2)}) collective-permute-start(bf16[192,128]{1,0:T(8,128)(2,1)} %get-tuple-element.18), channel_id=1, source_target_pairs={{0,96},{32,64},{64,32},{96,0},{1,97},{33,65},{65,33},{97,1},{2,98}... | collective-permute-start | bytes 147464 | tf_op jit(solution)/shard_map/ppermute | solution.py:695
  21.6 1.6 %collective-permute-start.3 = (bf16[96,128]{1,0:T(8,128)(2,1)}, bf16[96,128]{1,0:T(8,128)(2,1)S(1)}, u32[]{:S(2)}, u32[]{:S(2)}) collective-permute-start(bf16[96,128]{1,0:T(8,128)(2,1)} %get-tuple-element.19), channel_id=1, source_target_pairs={{0,64},{32,96},{64,0},{96,32},{1,65},{33,97},{65,1},{97,33},{2,66}... | collective-permute-start | bytes 73736 | tf_op jit(solution)/shard_map/ppermute | solution.py:696
  23.2 10.8 %inner_rows.1 = (bf16[3,16,64,512]{3,2,1,0:T(8,128)(2,1)}, f32[3,4,64,512]{3,2,1,0:T(8,128)}, f32[192,128]{1,0:T(8,128)}) custom-call(bf16[3,128,8,256]{3,2,1,0:T(8,128)(2,1)} %coarse_hbm.3, bf16[3,64,16,512]{3,2,1,0:T(8,128)(2,1)} %skip_hbm.3, bf16[2,2,64,128]{3,2,1,0:T(8,128)(2,1)} %up_w_hbm.5, bf16[3,3,64,128]{3,2,1,0:T(8,128)(2,1)} %w1_hbm.1, ...), custom_call_target="tpu_custom_call" | custom-call | tf_op jit(solution)/shard_map/inner_rows/pallas_call | solution.py:702
  34.0 0.0 collective-permute-done.3.across_hbm
  34.0 0.0 copy-start.4
  34.0 0.0 collective-permute-done.2.far_hbm
  34.0 0.0 copy-start.3
  34.0 2.2 %collective-permute-done.one_hbm = bf16[25,64,128]{2,1,0:T(8,128)(2,1)S(1)} collective-permute-done((bf16[25,64,128]{2,1,0:T(8,128)(2,1)}, bf16[25,64,128]{2,1,0:T(8,128)(2,1)S(1)}, u32[]{:S(2)}, u32[]{:S(2)}) %collective-permute-start) | collective-permute-done | bytes 409632 | tf_op jit(solution)/shard_map/ppermute | solution.py:693
  36.3 0.0 copy-start.1
  36.3 0.0 collective-permute-done.1.two_hbm
  36.3 0.0 all-to-all-done.recv_hbm
  36.3 0.0 copy-start
  36.3 0.0 copy-done.4
  36.3 0.0 copy-done.3
  36.3 0.7 copy-done.1
  37.0 0.1 copy-done.2
  37.2 0.3 copy-done
  37.5 9.6 %edges_and_second.1 = (f32[3,8,16,512]{3,2,1,0:T(8,128)}, bf16[128,32,128]{2,1,0:T(8,128)(2,1)}) custom-call(bf16[3,16,64,512]{3,2,1,0:T(8,128)(2,1)} %get-tuple-element.12.first_hbm, f32[3,4,64,512]{3,2,1,0:T(8,128)} %get-tuple-element.13.part_hbm, f32[192,128]{1,0:T(8,128)} %get-tuple-element.14.cols_hbm, bf16[25,64,128]{2,1,0:T(8,128)(2,1)} %copy-done.1, ...), custom_call_target="tpu_custom_call" | custom-call | tf_op jit(solution)/shard_map/edges_and_second/pallas_call | solution.py:724
  47.0 31.7 %all_to_all.10.recv_ref = bf16[128,32,128]{2,1,0:T(8,128)(2,1)S(1)} all-to-all(bf16[128,32,128]{2,1,0:T(8,128)(2,1)} %get-tuple-element.21), channel_id=1, replica_groups=mesh['face'=4,'tile'=32] {'face','tile'}, dimensions={0} | all-to-all | bytes 2097152 | tf_op jit(solution)/shard_map/all_to_all | solution.py:764
  78.7 1.5 %ocean_slots.1 = f32[44,24,128]{2,1,0:T(8,128)} custom-call(bf16[128,32,128]{2,1,0:T(8,128)(2,1)S(1)} %all_to_all.10.recv_ref), custom_call_target="tpu_custom_call" | custom-call | tf_op jit(solution)/shard_map/ocean_slots/pallas_call | solution.py:765
  (1 shorter events, 0.0 us)
Async XLA Ops:
  7.4 28.9 %all-to-all-start = ((bf16[32,96,128]{2,1,0:T(8,128)(2,1)}), bf16[32,96,128]{2,1,0:T(8,128)(2,1)S(1)}, u32[]{:S(2)}, u32[]{:S(2)}) async-start(bf16[32,96,128]{2,1,0:T(8,128)(2,1)} %get-tuple-element.17), calls=%async_computation | async-start | bytes 1572864 | tf_op jit(solution)/shard_map/all_to_all | solution.py:700
  16.7 19.6 %collective-permute-start = (bf16[25,64,128]{2,1,0:T(8,128)(2,1)}, bf16[25,64,128]{2,1,0:T(8,128)(2,1)S(1)}, u32[]{:S(2)}, u32[]{:S(2)}) collective-permute-start(bf16[25,64,128]{2,1,0:T(8,128)(2,1)} %get-tuple-element.15), channel_id=1, source_target_pairs={{0,1},{1,0},{2,3},{3,2},{4,5},{5,4},{6,7},{7,6},{8,9},{9,8},{10,11... | collective-permute-start | bytes 1228808 | tf_op jit(solution)/shard_map/ppermute | solution.py:693
  18.6 17.7 %collective-permute-start.1 = (bf16[25,64,128]{2,1,0:T(8,128)(2,1)}, bf16[25,64,128]{2,1,0:T(8,128)(2,1)S(1)}, u32[]{:S(2)}, u32[]{:S(2)}) collective-permute-start(bf16[25,64,128]{2,1,0:T(8,128)(2,1)} %get-tuple-element.16), channel_id=1, source_target_pairs={{1,2},{2,1},{3,4},{4,3},{5,6},{6,5},{7,8},{8,7},{9,10},{10,9},{11,... | collective-permute-start | bytes 1228808 | tf_op jit(solution)/shard_map/ppermute | solution.py:694
  20.1 14.0 %collective-permute-start.2 = (bf16[192,128]{1,0:T(8,128)(2,1)}, bf16[192,128]{1,0:T(8,128)(2,1)S(1)}, u32[]{:S(2)}, u32[]{:S(2)}) collective-permute-start(bf16[192,128]{1,0:T(8,128)(2,1)} %get-tuple-element.18), channel_id=1, source_target_pairs={{0,96},{32,64},{64,32},{96,0},{1,97},{33,65},{65,33},{97,1},{2,98}... | collective-permute-start | bytes 147464 | tf_op jit(solution)/shard_map/ppermute | solution.py:695
  21.6 12.4 %collective-permute-start.3 = (bf16[96,128]{1,0:T(8,128)(2,1)}, bf16[96,128]{1,0:T(8,128)(2,1)S(1)}, u32[]{:S(2)}, u32[]{:S(2)}) collective-permute-start(bf16[96,128]{1,0:T(8,128)(2,1)} %get-tuple-element.19), channel_id=1, source_target_pairs={{0,64},{32,96},{64,0},{96,32},{1,65},{33,97},{65,1},{97,33},{2,66}... | collective-permute-start | bytes 73736 | tf_op jit(solution)/shard_map/ppermute | solution.py:696
  34.0 2.3 %copy-start.4 = (bf16[96,128]{1,0:T(8,128)(2,1)}, bf16[96,128]{1,0:T(8,128)(2,1)S(1)}, u32[]{:S(2)}) copy-start(bf16[96,128]{1,0:T(8,128)(2,1)S(1)} %collective-permute-done.3.across_hbm) | copy-start | bytes 73732
  34.0 2.3 %copy-start.3 = (bf16[192,128]{1,0:T(8,128)(2,1)}, bf16[192,128]{1,0:T(8,128)(2,1)S(1)}, u32[]{:S(2)}) copy-start(bf16[192,128]{1,0:T(8,128)(2,1)S(1)} %collective-permute-done.2.far_hbm) | copy-start | bytes 147460
  36.3 0.8 copy-start.1
  36.3 0.9 %copy-start.2 = (bf16[25,64,128]{2,1,0:T(8,128)(2,1)}, bf16[25,64,128]{2,1,0:T(8,128)(2,1)S(1)}, u32[]{:S(2)}) copy-start(bf16[25,64,128]{2,1,0:T(8,128)(2,1)S(1)} %collective-permute-done.1.two_hbm) | copy-start | bytes 1228804
  36.3 1.2 %copy-start = (bf16[32,96,128]{2,1,0:T(8,128)(2,1)}, bf16[32,96,128]{2,1,0:T(8,128)(2,1)S(1)}, u32[]{:S(2)}) copy-start(bf16[32,96,128]{2,1,0:T(8,128)(2,1)S(1)} %all-to-all-done.recv_hbm) | copy-start | bytes 2359300

commit v5 on v4

--- a/solution.py
+++ b/solution.py
@@ -361,6 +361,11 @@
         pltpu.make_async_copy(source, target, sems.at[2, k])
         for k, (source, target) in enumerate(
             [
+                (one_hbm, one_ref),
+                (two_hbm, two_ref),
+                (across_hbm, across_ref),
+                (far_hbm, far_ref),
+                (recv_hbm.at[31], recv_ref.at[31]),
                 (up_w_hbm, up_w_ref),
                 (w1_hbm, w1_ref),
                 (w2_hbm, w2_ref),
@@ -372,11 +377,6 @@
                 (mask_hbm, mask_ref),
                 (target_hbm, target_ref),
                 (cols_hbm, cols_ref),
-                (one_hbm, one_ref),
-                (two_hbm, two_ref),
-                (across_hbm, across_ref),
-                (far_hbm, far_ref),
-                (recv_hbm.at[31], recv_ref.at[31]),
             ]
         )
     ]
@@ -393,8 +393,8 @@
 
     begin(small)
     begin(loads(0))
+    begin(loads(1))
     finish(small)
-    begin(loads(1))
     begin(loads(2))
 
     @pl.when(bottom)

time: 80.6 us -> 80.6 us (level)
  no operation moved by 1% of the time
where the time goes in v5:
time: 80.6 us; the launch traced here: 80.3 us
  blocking collectives  31.9 us (40%)
  Pallas kernels  28.5 us (35%)
  starting transfers between devices  15.8 us (20%)
  waiting for transfers between devices  2.26 us (3%)
  local copies, waits for them, and re-layouts  1.13 us (1%)
    all_to_all x1, blocking collectives, shards(): got = lax.all_to_all(send, both, 0, 0, tiled=True)  31.9 us
    pallas_call x1, Pallas kernels, shards(): pl.pallas_call(inner_kernel, in_specs=hbm(6), out_specs=hbm(3), out_shape...  10.8 us
    pallas_call x1, Pallas kernels, shards(): pl.pallas_call(edge_kernel, in_specs=hbm(18), out_specs=hbm(2), out_shape...  9.44 us
    all_to_all x1, starting transfers between devices, shards(): lax.all_to_all(send, both, 0, 0, axis_index_groups=groups, tiled=True)  9.27 us
    pallas_call x1, Pallas kernels, shards(): pl.pallas_call(pack_kernel, in_specs=hbm(5), out_specs=hbm(3) + vmem(2),...  6.81 us
    ppermute x1, waiting for transfers between devices, shards(): got_one = lax.ppermute(one, both, first_pairs)  2.25 us
    ppermute x1, starting transfers between devices, shards(): got_one = lax.ppermute(one, both, first_pairs)  1.87 us
  transfers between devices with their start and end apart: 5, of which 1 were waited for; matrix products, arithmetic and copies ran while one was open for 0% of the time, Pallas kernels for 13%

profile of v5, /device:TPU:0, one launch (start us, length us, event | category | flops | bytes accessed | tf_op | source)
XLA Modules:
  0.0 80.3 jit_solution(18259185022326772637)
XLA Ops:
  0.6 6.8 %pack_edges.1 = (bf16[25,64,128]{2,1,0:T(8,128)(2,1)}, bf16[25,64,128]{2,1,0:T(8,128)(2,1)}, bf16[32,96,128]{2,1,0:T(8,128)(2,1)}, bf16[96,128]{1,0:T(8,128)(2,1)}, bf16[192,128]{1,0:T(8,128)(2,1)}) custom-call(bf16[3,128,8,256]{3,2,1,0:T(8,128)(2,1)} %coarse_hbm.3, bf16[3,64,16,512]{3,2,1,0:T(8,128)(2,1)} %skip_hbm.3, bf16[2,2,64,128]{3,2,1,0:T(8,128)(2,1)} %up_w_hbm.5, ...), custom_call_target="tpu_custom_call" | custom-call | tf_op jit(solution)/shard_map/pack_edges/pallas_call | solution.py:655
  7.4 9.3 %all-to-all-start = ((bf16[32,96,128]{2,1,0:T(8,128)(2,1)}), bf16[32,96,128]{2,1,0:T(8,128)(2,1)S(1)}, u32[]{:S(2)}, u32[]{:S(2)}) async-start(bf16[32,96,128]{2,1,0:T(8,128)(2,1)} %get-tuple-element.17), calls=%async_computation | async-start | bytes 1572864 | tf_op jit(solution)/shard_map/all_to_all | solution.py:700
  16.7 1.9 %collective-permute-start = (bf16[25,64,128]{2,1,0:T(8,128)(2,1)}, bf16[25,64,128]{2,1,0:T(8,128)(2,1)S(1)}, u32[]{:S(2)}, u32[]{:S(2)}) collective-permute-start(bf16[25,64,128]{2,1,0:T(8,128)(2,1)} %get-tuple-element.15), channel_id=1, source_target_pairs={{0,1},{1,0},{2,3},{3,2},{4,5},{5,4},{6,7},{7,6},{8,9},{9,8},{10,11... | collective-permute-start | bytes 1228808 | tf_op jit(solution)/shard_map/ppermute | solution.py:693
  18.6 1.5 %collective-permute-start.1 = (bf16[25,64,128]{2,1,0:T(8,128)(2,1)}, bf16[25,64,128]{2,1,0:T(8,128)(2,1)S(1)}, u32[]{:S(2)}, u32[]{:S(2)}) collective-permute-start(bf16[25,64,128]{2,1,0:T(8,128)(2,1)} %get-tuple-element.16), channel_id=1, source_target_pairs={{1,2},{2,1},{3,4},{4,3},{5,6},{6,5},{7,8},{8,7},{9,10},{10,9},{11,... | collective-permute-start | bytes 1228808 | tf_op jit(solution)/shard_map/ppermute | solution.py:694
  20.1 1.5 %collective-permute-start.2 = (bf16[192,128]{1,0:T(8,128)(2,1)}, bf16[192,128]{1,0:T(8,128)(2,1)S(1)}, u32[]{:S(2)}, u32[]{:S(2)}) collective-permute-start(bf16[192,128]{1,0:T(8,128)(2,1)} %get-tuple-element.18), channel_id=1, source_target_pairs={{0,96},{32,64},{64,32},{96,0},{1,97},{33,65},{65,33},{97,1},{2,98}... | collective-permute-start | bytes 147464 | tf_op jit(solution)/shard_map/ppermute | solution.py:695
  21.6 1.6 %collective-permute-start.3 = (bf16[96,128]{1,0:T(8,128)(2,1)}, bf16[96,128]{1,0:T(8,128)(2,1)S(1)}, u32[]{:S(2)}, u32[]{:S(2)}) collective-permute-start(bf16[96,128]{1,0:T(8,128)(2,1)} %get-tuple-element.19), channel_id=1, source_target_pairs={{0,64},{32,96},{64,0},{96,32},{1,65},{33,97},{65,1},{97,33},{2,66}... | collective-permute-start | bytes 73736 | tf_op jit(solution)/shard_map/ppermute | solution.py:696
  23.2 10.8 %inner_rows.1 = (bf16[3,16,64,512]{3,2,1,0:T(8,128)(2,1)}, f32[3,4,64,512]{3,2,1,0:T(8,128)}, f32[192,128]{1,0:T(8,128)}) custom-call(bf16[3,128,8,256]{3,2,1,0:T(8,128)(2,1)} %coarse_hbm.3, bf16[3,64,16,512]{3,2,1,0:T(8,128)(2,1)} %skip_hbm.3, bf16[2,2,64,128]{3,2,1,0:T(8,128)(2,1)} %up_w_hbm.5, bf16[3,3,64,128]{3,2,1,0:T(8,128)(2,1)} %w1_hbm.1, ...), custom_call_target="tpu_custom_call" | custom-call | tf_op jit(solution)/shard_map/inner_rows/pallas_call | solution.py:702
  34.0 0.0 collective-permute-done.3.across_hbm
  34.0 0.0 copy-start.4
  34.0 0.0 collective-permute-done.2.far_hbm
  34.0 0.0 copy-start.3
  34.0 2.2 %collective-permute-done.one_hbm = bf16[25,64,128]{2,1,0:T(8,128)(2,1)S(1)} collective-permute-done((bf16[25,64,128]{2,1,0:T(8,128)(2,1)}, bf16[25,64,128]{2,1,0:T(8,128)(2,1)S(1)}, u32[]{:S(2)}, u32[]{:S(2)}) %collective-permute-start) | collective-permute-done | bytes 409632 | tf_op jit(solution)/shard_map/ppermute | solution.py:693
  36.3 0.0 copy-start.1
  36.3 0.0 collective-permute-done.1.two_hbm
  36.3 0.0 all-to-all-done.recv_hbm
  36.3 0.0 copy-start
  36.3 0.0 copy-done.4
  36.3 0.0 copy-done.3
  36.3 0.7 copy-done.1
  37.0 0.1 copy-done.2
  37.2 0.3 copy-done
  37.5 9.4 %edges_and_second.1 = (f32[3,8,16,512]{3,2,1,0:T(8,128)}, bf16[128,32,128]{2,1,0:T(8,128)(2,1)}) custom-call(bf16[3,16,64,512]{3,2,1,0:T(8,128)(2,1)} %get-tuple-element.12.first_hbm, f32[3,4,64,512]{3,2,1,0:T(8,128)} %get-tuple-element.13.part_hbm, f32[192,128]{1,0:T(8,128)} %get-tuple-element.14.cols_hbm, bf16[25,64,128]{2,1,0:T(8,128)(2,1)} %copy-done.1, ...), custom_call_target="tpu_custom_call" | custom-call | tf_op jit(solution)/shard_map/edges_and_second/pallas_call | solution.py:724
  46.9 31.9 %all_to_all.10.recv_ref = bf16[128,32,128]{2,1,0:T(8,128)(2,1)S(1)} all-to-all(bf16[128,32,128]{2,1,0:T(8,128)(2,1)} %get-tuple-element.21), channel_id=1, replica_groups=mesh['face'=4,'tile'=32] {'face','tile'}, dimensions={0} | all-to-all | bytes 2097152 | tf_op jit(solution)/shard_map/all_to_all | solution.py:764
  78.8 1.5 %ocean_slots.1 = f32[44,24,128]{2,1,0:T(8,128)} custom-call(bf16[128,32,128]{2,1,0:T(8,128)(2,1)S(1)} %all_to_all.10.recv_ref), custom_call_target="tpu_custom_call" | custom-call | tf_op jit(solution)/shard_map/ocean_slots/pallas_call | solution.py:765
  (1 shorter events, 0.0 us)
Async XLA Ops:
  7.4 28.9 %all-to-all-start = ((bf16[32,96,128]{2,1,0:T(8,128)(2,1)}), bf16[32,96,128]{2,1,0:T(8,128)(2,1)S(1)}, u32[]{:S(2)}, u32[]{:S(2)}) async-start(bf16[32,96,128]{2,1,0:T(8,128)(2,1)} %get-tuple-element.17), calls=%async_computation | async-start | bytes 1572864 | tf_op jit(solution)/shard_map/all_to_all | solution.py:700
  16.7 19.6 %collective-permute-start = (bf16[25,64,128]{2,1,0:T(8,128)(2,1)}, bf16[25,64,128]{2,1,0:T(8,128)(2,1)S(1)}, u32[]{:S(2)}, u32[]{:S(2)}) collective-permute-start(bf16[25,64,128]{2,1,0:T(8,128)(2,1)} %get-tuple-element.15), channel_id=1, source_target_pairs={{0,1},{1,0},{2,3},{3,2},{4,5},{5,4},{6,7},{7,6},{8,9},{9,8},{10,11... | collective-permute-start | bytes 1228808 | tf_op jit(solution)/shard_map/ppermute | solution.py:693
  18.6 17.7 %collective-permute-start.1 = (bf16[25,64,128]{2,1,0:T(8,128)(2,1)}, bf16[25,64,128]{2,1,0:T(8,128)(2,1)S(1)}, u32[]{:S(2)}, u32[]{:S(2)}) collective-permute-start(bf16[25,64,128]{2,1,0:T(8,128)(2,1)} %get-tuple-element.16), channel_id=1, source_target_pairs={{1,2},{2,1},{3,4},{4,3},{5,6},{6,5},{7,8},{8,7},{9,10},{10,9},{11,... | collective-permute-start | bytes 1228808 | tf_op jit(solution)/shard_map/ppermute | solution.py:694
  20.1 14.0 %collective-permute-start.2 = (bf16[192,128]{1,0:T(8,128)(2,1)}, bf16[192,128]{1,0:T(8,128)(2,1)S(1)}, u32[]{:S(2)}, u32[]{:S(2)}) collective-permute-start(bf16[192,128]{1,0:T(8,128)(2,1)} %get-tuple-element.18), channel_id=1, source_target_pairs={{0,96},{32,64},{64,32},{96,0},{1,97},{33,65},{65,33},{97,1},{2,98}... | collective-permute-start | bytes 147464 | tf_op jit(solution)/shard_map/ppermute | solution.py:695
  21.6 12.4 %collective-permute-start.3 = (bf16[96,128]{1,0:T(8,128)(2,1)}, bf16[96,128]{1,0:T(8,128)(2,1)S(1)}, u32[]{:S(2)}, u32[]{:S(2)}) collective-permute-start(bf16[96,128]{1,0:T(8,128)(2,1)} %get-tuple-element.19), channel_id=1, source_target_pairs={{0,64},{32,96},{64,0},{96,32},{1,65},{33,97},{65,1},{97,33},{2,66}... | collective-permute-start | bytes 73736 | tf_op jit(solution)/shard_map/ppermute | solution.py:696
  34.0 2.3 %copy-start.4 = (bf16[96,128]{1,0:T(8,128)(2,1)}, bf16[96,128]{1,0:T(8,128)(2,1)S(1)}, u32[]{:S(2)}) copy-start(bf16[96,128]{1,0:T(8,128)(2,1)S(1)} %collective-permute-done.3.across_hbm) | copy-start | bytes 73732
  34.0 2.3 %copy-start.3 = (bf16[192,128]{1,0:T(8,128)(2,1)}, bf16[192,128]{1,0:T(8,128)(2,1)S(1)}, u32[]{:S(2)}) copy-start(bf16[192,128]{1,0:T(8,128)(2,1)S(1)} %collective-permute-done.2.far_hbm) | copy-start | bytes 147460
  36.3 0.8 copy-start.1
  36.3 0.9 %copy-start.2 = (bf16[25,64,128]{2,1,0:T(8,128)(2,1)}, bf16[25,64,128]{2,1,0:T(8,128)(2,1)S(1)}, u32[]{:S(2)}) copy-start(bf16[25,64,128]{2,1,0:T(8,128)(2,1)S(1)} %collective-permute-done.1.two_hbm) | copy-start | bytes 1228804
  36.3 1.2 %copy-start = (bf16[32,96,128]{2,1,0:T(8,128)(2,1)}, bf16[32,96,128]{2,1,0:T(8,128)(2,1)S(1)}, u32[]{:S(2)}) copy-start(bf16[32,96,128]{2,1,0:T(8,128)(2,1)S(1)} %all-to-all-done.recv_hbm) | copy-start | bytes 2359300
